TPU v7x, 512 devices: a whole 4x4x16 slice. The times are simulated.
512 devices in a mesh: seq: 64 (over y, z), tensor: 8 (over x, core).
Axes of the slice: x: 4, y: 4, z: 16, core: 2. Of those that a mesh axis runs over, the one named last changes fastest.
Arguments:
- queries: bfloat16 [8192, 8192], P('seq', 'tensor'), may hold values from -360 to 360
- hidden: bfloat16 [8192, 8192], P('seq', 'tensor'), may hold values from -6 to 6
- key_value_weight: bfloat16 [2, 8192, 1024], P(None, 'tensor', 'seq'), may hold values from -0.0625 to 0.0625
- key_value_bias: bfloat16 [2, 1024], P(None, 'tensor'), may hold values from -3 to 3
- positions: int32 [3, 8192], P(None, 'seq'), may hold values from 0 to 78, as said below
- sink_index: int32 [512], replicated, may hold values from 0 to 8191, as said below
Outputs:
- attended: bfloat16 [8192, 8192], P('seq', 'tensor')
Inputs may be any that keep to these rules, and one draw needn't show every extreme that they name: `positions`: rows are the temporal, height and width ids; tokens come in frames of 16 x 16; within a frame the temporal id is fixed, and the height and width ids are the temporal id plus the token's row and column in the frame. `sink_index`: 512 distinct token indices in increasing order, 0 and 8191 among them.
All inputs are finite; a program needn't handle non-finite values.
Results may differ from a plain program's by a relative error of at most 0.012.
The roundings to bfloat16 on the way count: a program that leaves them out, or rounds other values in their place, can miss the bound.
Values may be sent and summed in bfloat16 or wider, within the bound.
A program may use at most 128 MiB of HBM per device.

v0:
```python
import math

import jax
import jax.numpy as jnp
from jax import lax
from jax.sharding import PartitionSpec as P

H = 64
KVH = 8
HD = 128
W = 4096


def shifted(array, axis, by):
    length = lax.axis_size(axis)
    pairs = [(i, i + by) for i in range(length) if 0 <= i + by < length]
    return lax.ppermute(array, axis, pairs)


def rope_tables(positions):
    half_width = HD // 2
    pair_index = jnp.arange(half_width, dtype=jnp.int32)
    inverse = jnp.exp(pair_index.astype(jnp.float32) * (-2.0 * math.log(1000000.0) / HD))
    first_cut = HD // 8
    second = first_cut + 3 * HD // 16
    chosen = jnp.where(
        pair_index[None, :] < first_cut,
        positions[0][:, None],
        jnp.where(pair_index[None, :] < second, positions[1][:, None], positions[2][:, None]),
    )
    angles = chosen.astype(jnp.float32) * inverse[None, :]
    angles = jnp.concatenate([angles, angles], axis=1)
    return (jnp.cos(angles), jnp.sin(angles))


def rotate(vectors, cosine_table, sine_table):
    half_width = HD // 2
    turned = jnp.concatenate([-vectors[..., half_width:], vectors[..., :half_width]], axis=-1)
    return vectors * cosine_table[:, None, :] + turned * sine_table[:, None, :]


def local(queries, hidden, key_value_weight, key_value_bias, positions, sink_index):
    row_count = hidden.shape[0]
    local_heads = key_value_bias.shape[1] // HD
    group_size = H // KVH
    my_index = lax.axis_index("seq")
    first_row = my_index * row_count
    scale = HD ** (-0.5)
    partial_sums = jnp.einsum(
        "td,cdn->tcn",
        hidden,
        lax.all_gather(key_value_weight, "seq", axis=2, tiled=True),
        preferred_element_type=jnp.float32,
    )
    partial_sums = partial_sums.reshape(row_count, 2, KVH, HD)
    summed = lax.psum_scatter(partial_sums, "tensor", scatter_dimension=2, tiled=True)
    summed = summed + key_value_bias.astype(jnp.float32).reshape(1, 2, local_heads, HD)
    cosine_table, sine_table = rope_tables(positions)
    rotated_keys = rotate(summed[:, 0], cosine_table, sine_table).astype(jnp.bfloat16)
    values = summed[:, 1].astype(jnp.bfloat16)
    own_block = jnp.stack([rotated_keys, values], axis=1)
    rotated_queries = rotate(
        queries.astype(jnp.float32).reshape(row_count, local_heads * group_size, HD),
        cosine_table,
        sine_table,
    ).astype(jnp.bfloat16)
    rotated_queries = rotated_queries.reshape(row_count, local_heads, group_size, HD)
    query_pos = first_row + jnp.arange(row_count, dtype=jnp.int32)
    onehot = (sink_index[:, None] == query_pos[None, :]).astype(jnp.bfloat16)
    picked = jnp.einsum("nt,tcjd->ncjd", onehot, own_block, preferred_element_type=jnp.float32)
    sink_block = lax.psum(picked, "seq").astype(jnp.bfloat16)

    def attend(carried, key_block, allowed):
        running_max, running_sum, running_out = carried
        scores = (
            jnp.einsum(
                "tkgd,lkd->kgtl",
                rotated_queries,
                key_block[:, 0],
                preferred_element_type=jnp.float32,
            )
            * scale
        )
        scores = jnp.where(allowed[None, None], scores, -1e30)
        new_max = jnp.maximum(running_max, scores.max(-1))
        factor = jnp.exp(running_max - new_max)
        weights = jnp.exp(scores - new_max[..., None])
        running_sum = running_sum * factor + weights.sum(-1)
        running_out = running_out * jnp.transpose(factor, (2, 0, 1))[..., None] + jnp.einsum(
            "kgtl,lkd->tkgd",
            weights.astype(jnp.bfloat16),
            key_block[:, 1],
            preferred_element_type=jnp.float32,
        )
        return (new_max, running_sum, running_out)

    carried = (
        jnp.full((local_heads, group_size, row_count), -1e30, jnp.float32),
        jnp.zeros((local_heads, group_size, row_count), jnp.float32),
        jnp.zeros((row_count, local_heads, group_size, HD), jnp.float32),
    )
    local_rows = jnp.arange(row_count, dtype=jnp.int32)
    carried = attend(carried, own_block, local_rows[None, :] <= local_rows[:, None])
    window_shards = W // row_count
    for shards_back in range(1, window_shards + 1):
        arrived = shifted(own_block, "seq", shards_back)
        key_pos = first_row - shards_back * row_count + jnp.arange(row_count, dtype=jnp.int32)
        earlier_allowed = (key_pos[None, :] >= 0) & (key_pos[None, :] > query_pos[:, None] - W)
        carried = attend(carried, arrived, earlier_allowed)
    sink_allowed = sink_index[None, :] <= query_pos[:, None] - W
    carried = attend(carried, sink_block, sink_allowed)
    running_max, running_sum, running_out = carried
    normalized = running_out / jnp.transpose(running_sum, (2, 0, 1))[..., None]
    return normalized.reshape(row_count, local_heads * group_size * HD).astype(jnp.bfloat16)


def solution(mesh):
    placed = (
        P("seq", "tensor"),
        P("seq", "tensor"),
        P(None, "tensor", "seq"),
        P(None, "tensor"),
        P(None, "seq"),
        P(),
    )
    return jax.shard_map(
        local, mesh=mesh, in_specs=placed, out_specs=P("seq", "tensor"), check_vma=False
    )
```

profile of v0, /device:TPU:96, one launch (start us, length us, event | category | flops | bytes accessed | tf_op | source)
XLA Modules:
  0.0 692.2 jit_solution(13770710465628987400)
XLA Ops:
  6.5 0.7 all-gather.2.cloned.1.call-update
  7.3 1.0 convert_bitcast_fusion
  9.0 0.8 slice_bitcast_fusion.136
  10.6 0.5 compare_and_fusion.13
  11.1 0.5 compare_and_fusion.22
  12.4 146.5 %all-gather.2.cloned.1.call-done = bf16[2,1024,1024]{1,2,0:T(8,128)(2,1)} async-done(((bf16[2,1024,16]{1,2,0:T(8,128)(2,1)}), bf16[2,1024,1024]{1,2,0:T(8,128)(2,1)}) %all-gather.2.cloned.1.call-update) | async-done | bytes 4194320 | tf_op jit(solution)/shard_map/all_gather | solution.py:52
  159.0 4.4 fusion.309
  163.7 1.3 dynamic-slice
  165.5 71.9 %all-reduce.4.cloned.1.call-done = f32[128,2,8,128]{0,3,2,1:T(8,128)} async-done(((f32[128,2,8,128]{0,3,2,1:T(8,128)}), f32[128,2,8,128]{0,3,2,1:T(8,128)}) %all-reduce.4.cloned.1.call-update) | async-done | bytes 1048592
  237.4 1.7 dynamic-slice_add_fusion
  239.4 4.9 collective-permute-start.31
  244.3 1.3 collective-permute-start.30
  245.6 1.3 collective-permute-start.29
  246.9 7.1 %collective-permute-start.28 = (bf16[128,2,1,128]{0,3,2,1:T(8,128)(2,1)S(1)}, bf16[128,2,1,128]{0,3,2,1:T(8,128)(2,1)S(1)}, u32[]{:S(2)}, u32[]{:S(2)}) collective-permute-start(bf16[128,2,1,128]{0,3,2,1:T(8,128)(2,1)S(1)} %pad_maximum_fusion.2), channel_id=1, source_target_pairs={{0,232},{8,240},{16,248},{24,256},{32,264},{40,272},{48,280},{56,2... | collective-permute-start | bytes 196616 | tf_op jit(solution)/shard_map/ppermute | solution.py:17
  254.0 2.3 collective-permute-start.27
  256.6 276.4 %all-reduce.5 = bf16[512,2,1,128]{3,0,1,2:T(8,128)(2,1)S(1)} all-reduce(f32[512,2,1,128]{3,0,1,2:T(8,128)S(1)} %convolution_bitcast_fusion.1), channel_id=1, replica_groups=mesh['seq'=64,'tensor'=8] {'seq'}, use_global_device_ids=true, to_apply=%region_34.35 | all-reduce | flops 131072 | bytes 786432 | tf_op jit(solution)/shard_map/psum | solution.py:71
  533.9 1.3 collective-permute-start.26
  535.4 7.4 %collective-permute-start.25 = (bf16[128,2,1,128]{0,3,2,1:T(8,128)(2,1)S(1)}, bf16[128,2,1,128]{0,3,2,1:T(8,128)(2,1)S(1)}, u32[]{:S(2)}, u32[]{:S(2)}) collective-permute-start(bf16[128,2,1,128]{0,3,2,1:T(8,128)(2,1)S(1)} %pad_maximum_fusion.2), channel_id=1, source_target_pairs={{0,208},{8,216},{16,224},{24,232},{32,240},{40,248},{48,256},{56,2... | collective-permute-start | bytes 196616 | tf_op jit(solution)/shard_map/ppermute | solution.py:17
  543.1 1.3 collective-permute-start.24
  544.7 1.3 collective-permute-start.23
  546.3 1.3 collective-permute-start.22
  547.9 1.3 collective-permute-start.21
  549.5 1.3 collective-permute-start.20
  551.1 6.6 collective-permute-done.24
  557.7 1.3 collective-permute-start.19
  559.2 5.7 collective-permute-done.23
  564.9 9.9 %collective-permute-start.18 = (bf16[128,2,1,128]{0,3,2,1:T(8,128)(2,1)S(1)}, bf16[128,2,1,128]{0,3,2,1:T(8,128)(2,1)S(1)}, u32[]{:S(2)}, u32[]{:S(2)}) collective-permute-start(bf16[128,2,1,128]{0,3,2,1:T(8,128)(2,1)S(1)} %pad_maximum_fusion.2), channel_id=1, source_target_pairs={{0,152},{8,160},{16,168},{24,176},{32,184},{40,192},{48,200},{56,2... | collective-permute-start | bytes 196616 | tf_op jit(solution)/shard_map/ppermute | solution.py:17
  575.1 9.0 %collective-permute-start.17 = (bf16[128,2,1,128]{0,3,2,1:T(8,128)(2,1)S(1)}, bf16[128,2,1,128]{0,3,2,1:T(8,128)(2,1)S(1)}, u32[]{:S(2)}, u32[]{:S(2)}) collective-permute-start(bf16[128,2,1,128]{0,3,2,1:T(8,128)(2,1)S(1)} %pad_maximum_fusion.2), channel_id=1, source_target_pairs={{0,144},{8,152},{16,160},{24,168},{32,176},{40,184},{48,192},{56,2... | collective-permute-start | bytes 196616 | tf_op jit(solution)/shard_map/ppermute | solution.py:17
  584.4 5.0 collective-permute-start.16
  589.7 6.6 collective-permute-start.15
  596.6 7.6 %collective-permute-start.14 = (bf16[128,2,1,128]{0,3,2,1:T(8,128)(2,1)S(1)}, bf16[128,2,1,128]{0,3,2,1:T(8,128)(2,1)S(1)}, u32[]{:S(2)}, u32[]{:S(2)}) collective-permute-start(bf16[128,2,1,128]{0,3,2,1:T(8,128)(2,1)S(1)} %pad_maximum_fusion.2), channel_id=1, source_target_pairs={{0,120},{8,128},{16,136},{24,144},{32,152},{40,160},{48,168},{56,1... | collective-permute-start | bytes 196616 | tf_op jit(solution)/shard_map/ppermute | solution.py:17
  604.5 3.3 collective-permute-start.13
  608.1 1.3 collective-permute-start.12
  609.7 2.8 collective-permute-start.11
  612.8 1.3 collective-permute-start.10
  614.4 3.2 collective-permute-start.9
  617.9 12.8 %collective-permute-start.8 = (bf16[128,2,1,128]{0,3,2,1:T(8,128)(2,1)S(1)}, bf16[128,2,1,128]{0,3,2,1:T(8,128)(2,1)S(1)}, u32[]{:S(2)}, u32[]{:S(2)}) collective-permute-start(bf16[128,2,1,128]{0,3,2,1:T(8,128)(2,1)S(1)} %pad_maximum_fusion.2), channel_id=1, source_target_pairs={{0,72},{8,80},{16,88},{24,96},{32,104},{40,112},{48,120},{56,128},... | collective-permute-start | bytes 196616 | tf_op jit(solution)/shard_map/ppermute | solution.py:17
  630.9 1.9 collective-permute-start.7
  633.1 2.2 collective-permute-start.6
  635.6 9.1 %collective-permute-start.5 = (bf16[128,2,1,128]{0,3,2,1:T(8,128)(2,1)S(1)}, bf16[128,2,1,128]{0,3,2,1:T(8,128)(2,1)S(1)}, u32[]{:S(2)}, u32[]{:S(2)}) collective-permute-start(bf16[128,2,1,128]{0,3,2,1:T(8,128)(2,1)S(1)} %pad_maximum_fusion.2), channel_id=1, source_target_pairs={{0,48},{8,56},{16,64},{24,72},{32,80},{40,88},{48,96},{56,104},{64... | collective-permute-start | bytes 196616 | tf_op jit(solution)/shard_map/ppermute | solution.py:17
  645.0 4.4 collective-permute-start.4
  649.7 1.3 collective-permute-start.3
  651.3 3.1 collective-permute-start.2
  654.7 8.7 %collective-permute-start.1 = (bf16[128,2,1,128]{0,3,2,1:T(8,128)(2,1)S(1)}, bf16[128,2,1,128]{0,3,2,1:T(8,128)(2,1)S(1)}, u32[]{:S(2)}, u32[]{:S(2)}) collective-permute-start(bf16[128,2,1,128]{0,3,2,1:T(8,128)(2,1)S(1)} %pad_maximum_fusion.2), channel_id=1, source_target_pairs={{0,16},{8,24},{16,32},{24,40},{32,48},{40,56},{48,64},{56,72},{64,... | collective-permute-start | bytes 196616 | tf_op jit(solution)/shard_map/ppermute | solution.py:17
  663.7 2.1 collective-permute-start
  666.9 3.0 collective-permute-done
  682.7 1.8 fusion.103
  684.5 0.9 copy.220
  (218 shorter events, 24.2 us)
Async XLA Ops:
  6.5 152.5 %copy-start = (bf16[128,1024]{1,0:T(8,128)(2,1)S(1)}, bf16[128,1024]{1,0:T(8,128)(2,1)}, u32[]{:S(2)}) copy-start(bf16[128,1024]{1,0:T(8,128)(2,1)} %param.7) | copy-start | bytes 786436
  6.5 3.6 copy-start.2
  6.5 152.4 %all-gather.2.cloned.1.call-start = ((), (), s32[]{:S(2)}) async-start(), calls=%async_computation | async-start | bytes 4259840 | tf_op jit(solution)/shard_map/all_gather | solution.py:52
  7.3 230.1 %all-reduce.4.cloned.1.call-start = ((), (), s32[]{:S(2)}) async-start(), calls=%async_computation.1 | async-start | bytes 2097152
  12.4 151.0 %copy-start.3 = (bf16[2,128]{1,0:T(2,128)(2,1)S(1)}, bf16[2,128]{1,0:T(2,128)(2,1)}, u32[]{:S(2)}) copy-start(bf16[2,128]{1,0:T(2,128)(2,1)} %param.9) | copy-start | bytes 1540
  163.4 1.8 copy-start.1
  239.4 294.5 %collective-permute-start.31 = (bf16[128,2,1,128]{0,3,2,1:T(8,128)(2,1)S(1)}, bf16[128,2,1,128]{0,3,2,1:T(8,128)(2,1)S(1)}, u32[]{:S(2)}, u32[]{:S(2)}) collective-permute-start(bf16[128,2,1,128]{0,3,2,1:T(8,128)(2,1)S(1)} %pad_maximum_fusion.2), channel_id=1, source_target_pairs={{0,256},{8,264},{16,272},{24,280},{32,288},{40,296},{48,304},{56,3... | collective-permute-start | bytes 196616 | tf_op jit(solution)/shard_map/ppermute | solution.py:17
  244.3 291.1 %collective-permute-start.30 = (bf16[128,2,1,128]{0,3,2,1:T(8,128)(2,1)S(1)}, bf16[128,2,1,128]{0,3,2,1:T(8,128)(2,1)S(1)}, u32[]{:S(2)}, u32[]{:S(2)}) collective-permute-start(bf16[128,2,1,128]{0,3,2,1:T(8,128)(2,1)S(1)} %pad_maximum_fusion.2), channel_id=1, source_target_pairs={{0,248},{8,256},{16,264},{24,272},{32,280},{40,288},{48,296},{56,3... | collective-permute-start | bytes 196616 | tf_op jit(solution)/shard_map/ppermute | solution.py:17
  245.6 297.5 %collective-permute-start.29 = (bf16[128,2,1,128]{0,3,2,1:T(8,128)(2,1)S(1)}, bf16[128,2,1,128]{0,3,2,1:T(8,128)(2,1)S(1)}, u32[]{:S(2)}, u32[]{:S(2)}) collective-permute-start(bf16[128,2,1,128]{0,3,2,1:T(8,128)(2,1)S(1)} %pad_maximum_fusion.2), channel_id=1, source_target_pairs={{0,240},{8,248},{16,256},{24,264},{32,272},{40,280},{48,288},{56,2... | collective-permute-start | bytes 196616 | tf_op jit(solution)/shard_map/ppermute | solution.py:17
  246.9 297.8 %collective-permute-start.28 = (bf16[128,2,1,128]{0,3,2,1:T(8,128)(2,1)S(1)}, bf16[128,2,1,128]{0,3,2,1:T(8,128)(2,1)S(1)}, u32[]{:S(2)}, u32[]{:S(2)}) collective-permute-start(bf16[128,2,1,128]{0,3,2,1:T(8,128)(2,1)S(1)} %pad_maximum_fusion.2), channel_id=1, source_target_pairs={{0,232},{8,240},{16,248},{24,256},{32,264},{40,272},{48,280},{56,2... | collective-permute-start | bytes 196616 | tf_op jit(solution)/shard_map/ppermute | solution.py:17
  254.0 292.3 %collective-permute-start.27 = (bf16[128,2,1,128]{0,3,2,1:T(8,128)(2,1)S(1)}, bf16[128,2,1,128]{0,3,2,1:T(8,128)(2,1)S(1)}, u32[]{:S(2)}, u32[]{:S(2)}) collective-permute-start(bf16[128,2,1,128]{0,3,2,1:T(8,128)(2,1)S(1)} %pad_maximum_fusion.2), channel_id=1, source_target_pairs={{0,224},{8,232},{16,240},{24,248},{32,256},{40,264},{48,272},{56,2... | collective-permute-start | bytes 196616 | tf_op jit(solution)/shard_map/ppermute | solution.py:17
  533.9 14.0 %collective-permute-start.26 = (bf16[128,2,1,128]{0,3,2,1:T(8,128)(2,1)S(1)}, bf16[128,2,1,128]{0,3,2,1:T(8,128)(2,1)S(1)}, u32[]{:S(2)}, u32[]{:S(2)}) collective-permute-start(bf16[128,2,1,128]{0,3,2,1:T(8,128)(2,1)S(1)} %pad_maximum_fusion.2), channel_id=1, source_target_pairs={{0,216},{8,224},{16,232},{24,240},{32,248},{40,256},{48,264},{56,2... | collective-permute-start | bytes 196616 | tf_op jit(solution)/shard_map/ppermute | solution.py:17
  535.4 14.0 %collective-permute-start.25 = (bf16[128,2,1,128]{0,3,2,1:T(8,128)(2,1)S(1)}, bf16[128,2,1,128]{0,3,2,1:T(8,128)(2,1)S(1)}, u32[]{:S(2)}, u32[]{:S(2)}) collective-permute-start(bf16[128,2,1,128]{0,3,2,1:T(8,128)(2,1)S(1)} %pad_maximum_fusion.2), channel_id=1, source_target_pairs={{0,208},{8,216},{16,224},{24,232},{32,240},{40,248},{48,256},{56,2... | collective-permute-start | bytes 196616 | tf_op jit(solution)/shard_map/ppermute | solution.py:17
  543.1 14.5 %collective-permute-start.24 = (bf16[128,2,1,128]{0,3,2,1:T(8,128)(2,1)S(1)}, bf16[128,2,1,128]{0,3,2,1:T(8,128)(2,1)S(1)}, u32[]{:S(2)}, u32[]{:S(2)}) collective-permute-start(bf16[128,2,1,128]{0,3,2,1:T(8,128)(2,1)S(1)} %pad_maximum_fusion.2), channel_id=1, source_target_pairs={{0,200},{8,208},{16,216},{24,224},{32,232},{40,240},{48,248},{56,2... | collective-permute-start | bytes 196616 | tf_op jit(solution)/shard_map/ppermute | solution.py:17
  544.7 20.2 %collective-permute-start.23 = (bf16[128,2,1,128]{0,3,2,1:T(8,128)(2,1)S(1)}, bf16[128,2,1,128]{0,3,2,1:T(8,128)(2,1)S(1)}, u32[]{:S(2)}, u32[]{:S(2)}) collective-permute-start(bf16[128,2,1,128]{0,3,2,1:T(8,128)(2,1)S(1)} %pad_maximum_fusion.2), channel_id=1, source_target_pairs={{0,192},{8,200},{16,208},{24,216},{32,224},{40,232},{48,240},{56,2... | collective-permute-start | bytes 196616 | tf_op jit(solution)/shard_map/ppermute | solution.py:17
  546.3 28.8 %collective-permute-start.22 = (bf16[128,2,1,128]{0,3,2,1:T(8,128)(2,1)S(1)}, bf16[128,2,1,128]{0,3,2,1:T(8,128)(2,1)S(1)}, u32[]{:S(2)}, u32[]{:S(2)}) collective-permute-start(bf16[128,2,1,128]{0,3,2,1:T(8,128)(2,1)S(1)} %pad_maximum_fusion.2), channel_id=1, source_target_pairs={{0,184},{8,192},{16,200},{24,208},{32,216},{40,224},{48,232},{56,2... | collective-permute-start | bytes 196616 | tf_op jit(solution)/shard_map/ppermute | solution.py:17
  547.9 36.5 %collective-permute-start.21 = (bf16[128,2,1,128]{0,3,2,1:T(8,128)(2,1)S(1)}, bf16[128,2,1,128]{0,3,2,1:T(8,128)(2,1)S(1)}, u32[]{:S(2)}, u32[]{:S(2)}) collective-permute-start(bf16[128,2,1,128]{0,3,2,1:T(8,128)(2,1)S(1)} %pad_maximum_fusion.2), channel_id=1, source_target_pairs={{0,176},{8,184},{16,192},{24,200},{32,208},{40,216},{48,224},{56,2... | collective-permute-start | bytes 196616 | tf_op jit(solution)/shard_map/ppermute | solution.py:17
  549.5 40.2 %collective-permute-start.20 = (bf16[128,2,1,128]{0,3,2,1:T(8,128)(2,1)S(1)}, bf16[128,2,1,128]{0,3,2,1:T(8,128)(2,1)S(1)}, u32[]{:S(2)}, u32[]{:S(2)}) collective-permute-start(bf16[128,2,1,128]{0,3,2,1:T(8,128)(2,1)S(1)} %pad_maximum_fusion.2), channel_id=1, source_target_pairs={{0,168},{8,176},{16,184},{24,192},{32,200},{40,208},{48,216},{56,2... | collective-permute-start | bytes 196616 | tf_op jit(solution)/shard_map/ppermute | solution.py:17
  557.7 38.9 %collective-permute-start.19 = (bf16[128,2,1,128]{0,3,2,1:T(8,128)(2,1)S(1)}, bf16[128,2,1,128]{0,3,2,1:T(8,128)(2,1)S(1)}, u32[]{:S(2)}, u32[]{:S(2)}) collective-permute-start(bf16[128,2,1,128]{0,3,2,1:T(8,128)(2,1)S(1)} %pad_maximum_fusion.2), channel_id=1, source_target_pairs={{0,160},{8,168},{16,176},{24,184},{32,192},{40,200},{48,208},{56,2... | collective-permute-start | bytes 196616 | tf_op jit(solution)/shard_map/ppermute | solution.py:17
  564.9 39.6 %collective-permute-start.18 = (bf16[128,2,1,128]{0,3,2,1:T(8,128)(2,1)S(1)}, bf16[128,2,1,128]{0,3,2,1:T(8,128)(2,1)S(1)}, u32[]{:S(2)}, u32[]{:S(2)}) collective-permute-start(bf16[128,2,1,128]{0,3,2,1:T(8,128)(2,1)S(1)} %pad_maximum_fusion.2), channel_id=1, source_target_pairs={{0,152},{8,160},{16,168},{24,176},{32,184},{40,192},{48,200},{56,2... | collective-permute-start | bytes 196616 | tf_op jit(solution)/shard_map/ppermute | solution.py:17
  575.1 33.0 %collective-permute-start.17 = (bf16[128,2,1,128]{0,3,2,1:T(8,128)(2,1)S(1)}, bf16[128,2,1,128]{0,3,2,1:T(8,128)(2,1)S(1)}, u32[]{:S(2)}, u32[]{:S(2)}) collective-permute-start(bf16[128,2,1,128]{0,3,2,1:T(8,128)(2,1)S(1)} %pad_maximum_fusion.2), channel_id=1, source_target_pairs={{0,144},{8,152},{16,160},{24,168},{32,176},{40,184},{48,192},{56,2... | collective-permute-start | bytes 196616 | tf_op jit(solution)/shard_map/ppermute | solution.py:17
  584.4 25.3 %collective-permute-start.16 = (bf16[128,2,1,128]{0,3,2,1:T(8,128)(2,1)S(1)}, bf16[128,2,1,128]{0,3,2,1:T(8,128)(2,1)S(1)}, u32[]{:S(2)}, u32[]{:S(2)}) collective-permute-start(bf16[128,2,1,128]{0,3,2,1:T(8,128)(2,1)S(1)} %pad_maximum_fusion.2), channel_id=1, source_target_pairs={{0,136},{8,144},{16,152},{24,160},{32,168},{40,176},{48,184},{56,1... | collective-permute-start | bytes 196616 | tf_op jit(solution)/shard_map/ppermute | solution.py:17
  589.7 23.1 %collective-permute-start.15 = (bf16[128,2,1,128]{0,3,2,1:T(8,128)(2,1)S(1)}, bf16[128,2,1,128]{0,3,2,1:T(8,128)(2,1)S(1)}, u32[]{:S(2)}, u32[]{:S(2)}) collective-permute-start(bf16[128,2,1,128]{0,3,2,1:T(8,128)(2,1)S(1)} %pad_maximum_fusion.2), channel_id=1, source_target_pairs={{0,128},{8,136},{16,144},{24,152},{32,160},{40,168},{48,176},{56,1... | collective-permute-start | bytes 196616 | tf_op jit(solution)/shard_map/ppermute | solution.py:17
  596.6 17.8 %collective-permute-start.14 = (bf16[128,2,1,128]{0,3,2,1:T(8,128)(2,1)S(1)}, bf16[128,2,1,128]{0,3,2,1:T(8,128)(2,1)S(1)}, u32[]{:S(2)}, u32[]{:S(2)}) collective-permute-start(bf16[128,2,1,128]{0,3,2,1:T(8,128)(2,1)S(1)} %pad_maximum_fusion.2), channel_id=1, source_target_pairs={{0,120},{8,128},{16,136},{24,144},{32,152},{40,160},{48,168},{56,1... | collective-permute-start | bytes 196616 | tf_op jit(solution)/shard_map/ppermute | solution.py:17
  604.5 13.4 %collective-permute-start.13 = (bf16[128,2,1,128]{0,3,2,1:T(8,128)(2,1)S(1)}, bf16[128,2,1,128]{0,3,2,1:T(8,128)(2,1)S(1)}, u32[]{:S(2)}, u32[]{:S(2)}) collective-permute-start(bf16[128,2,1,128]{0,3,2,1:T(8,128)(2,1)S(1)} %pad_maximum_fusion.2), channel_id=1, source_target_pairs={{0,112},{8,120},{16,128},{24,136},{32,144},{40,152},{48,160},{56,1... | collective-permute-start | bytes 196616 | tf_op jit(solution)/shard_map/ppermute | solution.py:17
  608.1 22.8 %collective-permute-start.12 = (bf16[128,2,1,128]{0,3,2,1:T(8,128)(2,1)S(1)}, bf16[128,2,1,128]{0,3,2,1:T(8,128)(2,1)S(1)}, u32[]{:S(2)}, u32[]{:S(2)}) collective-permute-start(bf16[128,2,1,128]{0,3,2,1:T(8,128)(2,1)S(1)} %pad_maximum_fusion.2), channel_id=1, source_target_pairs={{0,104},{8,112},{16,120},{24,128},{32,136},{40,144},{48,152},{56,1... | collective-permute-start | bytes 196616 | tf_op jit(solution)/shard_map/ppermute | solution.py:17
  609.7 23.4 %collective-permute-start.11 = (bf16[128,2,1,128]{0,3,2,1:T(8,128)(2,1)S(1)}, bf16[128,2,1,128]{0,3,2,1:T(8,128)(2,1)S(1)}, u32[]{:S(2)}, u32[]{:S(2)}) collective-permute-start(bf16[128,2,1,128]{0,3,2,1:T(8,128)(2,1)S(1)} %pad_maximum_fusion.2), channel_id=1, source_target_pairs={{0,96},{8,104},{16,112},{24,120},{32,128},{40,136},{48,144},{56,15... | collective-permute-start | bytes 196616 | tf_op jit(solution)/shard_map/ppermute | solution.py:17
  612.8 22.8 %collective-permute-start.10 = (bf16[128,2,1,128]{0,3,2,1:T(8,128)(2,1)S(1)}, bf16[128,2,1,128]{0,3,2,1:T(8,128)(2,1)S(1)}, u32[]{:S(2)}, u32[]{:S(2)}) collective-permute-start(bf16[128,2,1,128]{0,3,2,1:T(8,128)(2,1)S(1)} %pad_maximum_fusion.2), channel_id=1, source_target_pairs={{0,88},{8,96},{16,104},{24,112},{32,120},{40,128},{48,136},{56,144... | collective-permute-start | bytes 196616 | tf_op jit(solution)/shard_map/ppermute | solution.py:17
  614.4 30.6 %collective-permute-start.9 = (bf16[128,2,1,128]{0,3,2,1:T(8,128)(2,1)S(1)}, bf16[128,2,1,128]{0,3,2,1:T(8,128)(2,1)S(1)}, u32[]{:S(2)}, u32[]{:S(2)}) collective-permute-start(bf16[128,2,1,128]{0,3,2,1:T(8,128)(2,1)S(1)} %pad_maximum_fusion.2), channel_id=1, source_target_pairs={{0,80},{8,88},{16,96},{24,104},{32,112},{40,120},{48,128},{56,136}... | collective-permute-start | bytes 196616 | tf_op jit(solution)/shard_map/ppermute | solution.py:17
  617.9 31.8 %collective-permute-start.8 = (bf16[128,2,1,128]{0,3,2,1:T(8,128)(2,1)S(1)}, bf16[128,2,1,128]{0,3,2,1:T(8,128)(2,1)S(1)}, u32[]{:S(2)}, u32[]{:S(2)}) collective-permute-start(bf16[128,2,1,128]{0,3,2,1:T(8,128)(2,1)S(1)} %pad_maximum_fusion.2), channel_id=1, source_target_pairs={{0,72},{8,80},{16,88},{24,96},{32,104},{40,112},{48,120},{56,128},... | collective-permute-start | bytes 196616 | tf_op jit(solution)/shard_map/ppermute | solution.py:17
  630.9 20.3 %collective-permute-start.7 = (bf16[128,2,1,128]{0,3,2,1:T(8,128)(2,1)S(1)}, bf16[128,2,1,128]{0,3,2,1:T(8,128)(2,1)S(1)}, u32[]{:S(2)}, u32[]{:S(2)}) collective-permute-start(bf16[128,2,1,128]{0,3,2,1:T(8,128)(2,1)S(1)} %pad_maximum_fusion.2), channel_id=1, source_target_pairs={{0,64},{8,72},{16,80},{24,88},{32,96},{40,104},{48,112},{56,120},{... | collective-permute-start | bytes 196616 | tf_op jit(solution)/shard_map/ppermute | solution.py:17
  633.1 21.5 %collective-permute-start.6 = (bf16[128,2,1,128]{0,3,2,1:T(8,128)(2,1)S(1)}, bf16[128,2,1,128]{0,3,2,1:T(8,128)(2,1)S(1)}, u32[]{:S(2)}, u32[]{:S(2)}) collective-permute-start(bf16[128,2,1,128]{0,3,2,1:T(8,128)(2,1)S(1)} %pad_maximum_fusion.2), channel_id=1, source_target_pairs={{0,56},{8,64},{16,72},{24,80},{32,88},{40,96},{48,104},{56,112},{6... | collective-permute-start | bytes 196616 | tf_op jit(solution)/shard_map/ppermute | solution.py:17
  635.6 28.1 %collective-permute-start.5 = (bf16[128,2,1,128]{0,3,2,1:T(8,128)(2,1)S(1)}, bf16[128,2,1,128]{0,3,2,1:T(8,128)(2,1)S(1)}, u32[]{:S(2)}, u32[]{:S(2)}) collective-permute-start(bf16[128,2,1,128]{0,3,2,1:T(8,128)(2,1)S(1)} %pad_maximum_fusion.2), channel_id=1, source_target_pairs={{0,48},{8,56},{16,64},{24,72},{32,80},{40,88},{48,96},{56,104},{64... | collective-permute-start | bytes 196616 | tf_op jit(solution)/shard_map/ppermute | solution.py:17
  645.0 21.0 %collective-permute-start.4 = (bf16[128,2,1,128]{0,3,2,1:T(8,128)(2,1)S(1)}, bf16[128,2,1,128]{0,3,2,1:T(8,128)(2,1)S(1)}, u32[]{:S(2)}, u32[]{:S(2)}) collective-permute-start(bf16[128,2,1,128]{0,3,2,1:T(8,128)(2,1)S(1)} %pad_maximum_fusion.2), channel_id=1, source_target_pairs={{0,40},{8,48},{16,56},{24,64},{32,72},{40,80},{48,88},{56,96},{64,... | collective-permute-start | bytes 196616 | tf_op jit(solution)/shard_map/ppermute | solution.py:17
  649.7 20.4 %collective-permute-start.3 = (bf16[128,2,1,128]{0,3,2,1:T(8,128)(2,1)S(1)}, bf16[128,2,1,128]{0,3,2,1:T(8,128)(2,1)S(1)}, u32[]{:S(2)}, u32[]{:S(2)}) collective-permute-start(bf16[128,2,1,128]{0,3,2,1:T(8,128)(2,1)S(1)} %pad_maximum_fusion.2), channel_id=1, source_target_pairs={{0,32},{8,40},{16,48},{24,56},{32,64},{40,72},{48,80},{56,88},{64,... | collective-permute-start | bytes 196616 | tf_op jit(solution)/shard_map/ppermute | solution.py:17
  651.3 15.1 %collective-permute-start.2 = (bf16[128,2,1,128]{0,3,2,1:T(8,128)(2,1)S(1)}, bf16[128,2,1,128]{0,3,2,1:T(8,128)(2,1)S(1)}, u32[]{:S(2)}, u32[]{:S(2)}) collective-permute-start(bf16[128,2,1,128]{0,3,2,1:T(8,128)(2,1)S(1)} %pad_maximum_fusion.2), channel_id=1, source_target_pairs={{0,24},{8,32},{16,40},{24,48},{32,56},{40,64},{48,72},{56,80},{64,... | collective-permute-start | bytes 196616 | tf_op jit(solution)/shard_map/ppermute | solution.py:17
  654.7 11.9 %collective-permute-start.1 = (bf16[128,2,1,128]{0,3,2,1:T(8,128)(2,1)S(1)}, bf16[128,2,1,128]{0,3,2,1:T(8,128)(2,1)S(1)}, u32[]{:S(2)}, u32[]{:S(2)}) collective-permute-start(bf16[128,2,1,128]{0,3,2,1:T(8,128)(2,1)S(1)} %pad_maximum_fusion.2), channel_id=1, source_target_pairs={{0,16},{8,24},{16,32},{24,40},{32,48},{40,56},{48,64},{56,72},{64,... | collective-permute-start | bytes 196616 | tf_op jit(solution)/shard_map/ppermute | solution.py:17
  663.7 6.2 collective-permute-start
Sparse Core Ops, SparseCore 0:
  10.3 148.6 all-gather.1
  163.6 73.7 all-reduce.3
where the time goes:
time: 693 us; the launch traced here: 692 us
  blocking collectives  276 us (40%)
  waiting for transfers between devices  235 us (34%)
  starting transfers between devices  129 us (19%)
  matrix products  23.8 us (3%)
  between operations  15.2 us (2%)
  other arithmetic  9.84 us (1%)
    psum x1, blocking collectives, local(): sink_block = lax.psum(picked, 'seq').astype(jnp.bfloat16)  276 us
    all_gather x1, waiting for transfers between devices, local(): lax.all_gather(key_value_weight, 'seq', axis=2, tiled=True)  147 us
    ppermute x32, starting transfers between devices, shifted(): return lax.ppermute(array, axis, pairs)  129 us
    unnamed x3, waiting for transfers between devices  72.7 us
    ppermute x32, waiting for transfers between devices, shifted(): return lax.ppermute(array, axis, pairs)  15.4 us
  transfers between devices with their start and end apart: 34, of which 5 were waited for; matrix products, arithmetic and copies ran while one was open for 2% of the time, Pallas kernels for 0%

commit v1 on v0

v1 whole, which is shorter than its diff:
```python
import functools
import math

import jax
import jax.numpy as jnp
from jax import lax
from jax.experimental import pallas as pl
from jax.experimental.pallas import tpu as pltpu
from jax.sharding import PartitionSpec as P

H = 64
KVH = 8
HD = 128
W = 4096
NX = 4
NY = 4
NZ = 16
NS = NY * NZ
TQ = 128
G = H // KVH
DL = 1024
NSINK = 512
MESH = pl.DeviceIdType.MESH
LOG2E = 1.4426950408889634
BF = jnp.bfloat16
F32 = jnp.float32


def coords():
    s = lax.axis_index("seq")
    t = lax.axis_index("tensor")
    return s, t, t // 2, t % 2, s // NZ, s % NZ


def remote(src, dst, send, recv, seq, tensor):
    return pltpu.make_async_remote_copy(
        src_ref=src,
        dst_ref=dst,
        send_sem=send,
        recv_sem=recv,
        device_id=(seq, tensor),
        device_id_type=MESH,
    )


def nt_dot(a, b):
    return lax.dot_general(a, b, (((1,), (1,)), ((), ())), preferred_element_type=F32)


def rope_tables(p_ref):
    row = lax.broadcasted_iota(jnp.int32, (HD, TQ), 0)
    pair = lax.rem(row, HD // 2)
    inverse = jnp.exp(pair.astype(F32) * (-2.0 * math.log(1000000.0) / HD))
    first = HD // 8
    second = first + 3 * HD // 16
    pos = p_ref[...]
    chosen = jnp.where(
        pair < first,
        jnp.broadcast_to(pos[0:1], (HD, TQ)),
        jnp.where(
            pair < second,
            jnp.broadcast_to(pos[1:2], (HD, TQ)),
            jnp.broadcast_to(pos[2:3], (HD, TQ)),
        ),
    )
    angles = chosen.astype(F32) * inverse
    cosine = jnp.cos(angles)
    sine = jnp.where(row < HD // 2, -jnp.sin(angles), jnp.sin(angles))
    return jnp.transpose(cosine), jnp.transpose(sine)


def rotate(u, cosine, sine):
    return u * cosine + pltpu.roll(u, HD // 2, 1) * sine


def project(
    q_ref, h_ref, w_ref, b_ref, p_ref, qo_ref, ko_ref, vo_ref,
    hid, wbuf, p3s, p3r, p4s, p4r, cos_ref, sin_ref,
    hs, hr, fs, fr, bs, br, p3ss, p3rs, p4ss, p4rs,
):
    s, t, x, c, y, z = coords()
    up, down = y * NZ + lax.rem(z + 1, NZ), y * NZ + lax.rem(z + NZ - 1, NZ)
    other = x * 2 + (1 - c)
    mine = x == y

    barrier = pltpu.get_barrier_semaphore()

    def greet(seq, tensor):
        pl.semaphore_signal(barrier, inc=1, device_id=(seq, tensor), device_id_type=MESH)

    greet(s, other)
    greet(up, t)
    greet(down, t)
    for d in range(1, NY):
        greet(lax.rem(y + d, NY) * NZ + z, t)
    for xs in range(NX):
        @pl.when(jnp.logical_not(mine & (x == xs)))
        def _(xs=xs):
            greet(x * NZ + z, xs * 2 + c)

    def w_rows(origin, kv):
        return wbuf.at[origin // 8, pl.ds(pl.multiple_of(kv * HD + lax.rem(origin, 8) * 16, 16), 16)]

    for kv in range(2):
        w_rows(z, kv)[...] = w_ref[kv]
    hid[y] = h_ref[...]
    pl.semaphore_wait(barrier, jnp.where(mine, 9, 10))

    def h_copy(d):
        return remote(h_ref, hid.at[y], hs.at[d], hr.at[d], lax.rem(y + d, NY) * NZ + z, t)

    def f_copy(k, kv):
        rows = w_rows(lax.rem(z - (k - 1) + NZ, NZ), kv)
        return remote(rows, rows, fs.at[k, kv], fr.at[k, kv], up, t)

    def b_copy(k, kv):
        rows = w_rows(lax.rem(z + (k - 1), NZ), kv)
        return remote(rows, rows, bs.at[k, kv], br.at[k, kv], down, t)

    def f_wait(k, kv):
        rows = w_rows(lax.rem(z - k + NZ, NZ), kv)
        remote(rows, rows, fs.at[k, kv], fr.at[k, kv], up, t).wait_recv()

    def b_wait(k, kv):
        rows = w_rows(lax.rem(z + k, NZ), kv)
        remote(rows, rows, bs.at[k, kv], br.at[k, kv], down, t).wait_recv()

    for kv in range(2):
        f_copy(1, kv).start()
        b_copy(1, kv).start()
    for d in (1, 3, 2):
        h_copy(d).start()

    cosine, sine = rope_tables(p_ref)
    cos_ref[...] = cosine
    sin_ref[...] = sine
    for k in range(2, 9):
        for kv in range(2):
            f_wait(k - 1, kv)
            f_copy(k, kv).start()
            b_wait(k - 1, kv)
            if k <= 7:
                b_copy(k, kv).start()
        for g in ([k - 2] if k < 8 else [6, 7]):
            u = q_ref[:, g * HD : (g + 1) * HD].astype(F32)
            qo_ref[g * TQ : (g + 1) * TQ, :] = rotate(u, cos_ref[...], sin_ref[...]).astype(BF)
    for d in range(1, NY):
        slot = hid.at[lax.rem(y + NY - d, NY)]
        remote(slot, slot, hs.at[d], hr.at[d], s, t).wait_recv()
    for kv in range(2):
        f_wait(8, kv)

    for i in range(NY):
        p3s[i] = nt_dot(hid[i], wbuf[1 - c])
        remote(p3s.at[i], p3r.at[i], p3ss.at[i], p3rs.at[i], s, other).start()
    for i in range(NY):
        p4s[i] = nt_dot(hid[i], wbuf[c])

    def p4_copy(i):
        return remote(p4s.at[i], p4r.at[x], p4ss.at[i], p4rs.at[x], i * NZ + z, y * 2 + c)

    for i in range(NY):
        remote(p3s.at[i], p3r.at[i], p3ss.at[i], p3rs.at[i], s, other).wait_recv()
        p4s[i] += p3r[i]

        @pl.when(mine & (y == i))
        def _(i=i):
            p4r[x] = p4s[i]

        @pl.when(jnp.logical_not(mine & (y == i)))
        def _(i=i):
            p4_copy(i).start()

    for xs in range(NX):
        @pl.when(jnp.logical_not(mine & (x == xs)))
        def _(xs=xs):
            remote(p4r.at[xs], p4r.at[xs], p4ss.at[xs], p4rs.at[xs], s, t).wait_recv()

    total = (p4r[0] + p4r[1]) + (p4r[2] + p4r[3])
    keys = total[:, :HD] + b_ref[0:1].astype(F32)
    ko_ref[...] = rotate(keys, cos_ref[...], sin_ref[...]).astype(BF)
    vo_ref[...] = (total[:, HD:] + b_ref[1:2].astype(F32)).astype(BF)

    for d in range(1, NY):
        h_copy(d).wait_send()
    for k in range(1, 9):
        for kv in range(2):
            f_copy(k, kv).wait_send()
            if k <= 7:
                b_copy(k, kv).wait_send()
    for i in range(NY):
        remote(p3s.at[i], p3r.at[i], p3ss.at[i], p3rs.at[i], s, other).wait_send()

        @pl.when(jnp.logical_not(mine & (y == i)))
        def _(i=i):
            p4_copy(i).wait_send()


def rounds():
    table = []
    for k in range(1, 9):
        waits = []
        back = 17 - k
        if k == 8:
            waits.append((32, [(-1, 31)]))
        if back > 8:
            waits.append((back, [(-1, back - 1)] if back > 9 else []))
        waits.append((k, ([(1, k + 1)] if k < 8 else []) + [(16, 16 + k)]))
        group = [k, back]
        if k >= 2:
            waits.append((15 + k, []))
            group.append(15 + k)
        table.append((waits, group))
    table.append(([(24, [(1, 25)]), (31, [(-1, 30)])], [24, 31, 32]))
    table.append(([(25, [(1, 26)]), (30, [(-1, 29)])], [25, 30]))
    table.append(([(26, [(1, 27)]), (29, [(-1, 28)])], [26, 29]))
    table.append(([(27, []), (28, [])], [27, 28]))
    return table


ROUNDS = rounds()
SLOT = {0: 0}
for _, group in ROUNDS:
    for j in group:
        SLOT[j] = len(SLOT)


def attention(
    q_ref, k_ref, v_ref, i_ref, o_ref,
    kbuf, vbuf, acc, m_ref, l_ref, sacc, sout, sin_a, sin_b, cs, cr, ss, sr,
):
    s, t, x, c, y, z = coords()

    def at(shift):
        return lax.rem(s + shift + NS, NS)

    barrier = pltpu.get_barrier_semaphore()
    for shift in (1, -1, 16, -16, 32):
        pl.semaphore_signal(barrier, inc=1, device_id=(at(shift), t), device_id_type=MESH)
    own = pl.ds(0, TQ)
    kbuf[own] = k_ref[...]
    vbuf[own] = v_ref[...]
    pl.semaphore_wait(barrier, 5)

    def rows(j):
        return pl.ds(SLOT[j] * TQ, TQ)

    def copy(kv, j, shift, there):
        buf = (kbuf, vbuf)[kv]
        return remote(buf.at[rows(j)], buf.at[rows(there)], cs.at[kv, there], cr.at[kv, there], at(shift), t)

    sends = []

    def send(kv, j, shift, there):
        copy(kv, j, shift, there).start()
        if kv == 0:
            sends.append((j, shift, there))

    for kv in range(2):
        send(kv, 0, 1, 1)
        send(kv, 0, 16, 16)
    for kv in range(2):
        send(kv, 0, 32, 32)

    scale = HD ** (-0.5) * LOG2E
    q_row = lax.broadcasted_iota(jnp.int32, (TQ, TQ), 0)
    k_col = lax.broadcasted_iota(jnp.int32, (TQ, TQ), 1)

    def attend(keys, values, count, masks, first=False):
        def body(g, carry):
            r = pl.ds(pl.multiple_of(g * TQ, TQ), TQ)
            scores = nt_dot(q_ref[r], keys[...]) * scale
            tiles = []
            for i in range(count):
                tile = scores[:, i * TQ : (i + 1) * TQ]
                if masks[i] is not None:
                    tile = jnp.where(masks[i](), tile, -1e30)
                tiles.append(tile)
            top = tiles[0]
            for tile in tiles[1:]:
                top = jnp.maximum(top, tile)
            top = jnp.broadcast_to(jnp.max(top, axis=1, keepdims=True), (TQ, TQ))
            if not first:
                old = m_ref[r]
                top = jnp.maximum(old, top)
                factor = jnp.exp2(old - top)
            m_ref[r] = top
            weights = [jnp.exp2(tile - top) for tile in tiles]
            summed = weights[0]
            for w in weights[1:]:
                summed = summed + w
            p = jnp.concatenate([w.astype(BF) for w in weights], axis=1) if count > 1 else weights[0].astype(BF)
            out = jnp.dot(p, values[...], preferred_element_type=F32)
            if first:
                l_ref[r] = summed
                acc[r] = out
            else:
                l_ref[r] = l_ref[r] * factor + summed
                acc[r] = acc[r] * factor + out
            return carry

        lax.fori_loop(0, G, body, 0, unroll=2)

    def mask_of(j):
        if j == 0:
            return lambda: k_col <= q_row
        if j == 32:
            return lambda: k_col > q_row
        return None

    def group_attend(group):
        n = len(group)
        start = SLOT[group[0]]
        span = pl.ds(start * TQ, n * TQ)

        @pl.when(s >= max(group))
        def _():
            attend(kbuf.at[span], vbuf.at[span], n, [mask_of(j) for j in group])

        @pl.when(s < max(group))
        def _():
            for j in group:
                @pl.when(s >= j)
                def _(j=j):
                    attend(kbuf.at[rows(j)], vbuf.at[rows(j)], 1, [mask_of(j)])

    sink_row = i_ref[...]

    def extract(j):
        base = (s - j) * TQ
        for i in range(NSINK // TQ):
            part = jnp.broadcast_to(sink_row[:, i * TQ : (i + 1) * TQ], (TQ, TQ)).astype(F32)
            column = jnp.transpose(part) - base.astype(F32)
            hot = jnp.where(column == k_col.astype(F32), 1.0, 0.0).astype(BF)
            r = pl.ds(i * TQ, TQ)
            for kv in range(2):
                picked = jnp.dot(hot, (kbuf, vbuf)[kv][rows(j)], preferred_element_type=F32)
                if j == 0:
                    sacc[kv, r] = picked
                else:
                    sacc[kv, r] += picked

    attend(kbuf.at[own], vbuf.at[own], 1, [mask_of(0)], first=True)

    @pl.when(y < 2)
    def _():
        extract(0)

    def sink_copy(dst, n, shift):
        return remote(sout, dst, ss.at[n], sr.at[n], at(shift), t)

    for index, (waits, group) in enumerate(ROUNDS):
        for kv in range(2):
            for j, onward in waits:
                copy(kv, j, 1, j).wait_recv()
                for shift, there in onward:
                    send(kv, j, shift, there)
        group_attend(group)
        for j in group:
            if j < 16:
                @pl.when((y < 2) & (s >= j))
                def _(j=j):
                    extract(j)
        if index == 7:
            @pl.when(y < 2)
            def _():
                sout[...] = sacc[...].astype(BF)

            @pl.when(y == 0)
            def _():
                sink_copy(sin_a, 0, 32).start()
                sink_copy(sin_a, 1, 48).start()

            @pl.when(y == 1)
            def _():
                sink_copy(sin_b, 2, 32).start()

    @pl.when(y == 2)
    def _():
        sink_copy(sin_a, 0, 32).wait_recv()

    @pl.when(y == 3)
    def _():
        sink_copy(sin_a, 1, 48).wait_recv()
        sink_copy(sin_b, 2, 32).wait_recv()
        sin_a[...] = sin_a[...] + sin_b[...]

    @pl.when(y >= 2)
    def _():
        def sink_mask(i):
            return lambda: sink_row[:, i * TQ : (i + 1) * TQ] <= q_row + (s * TQ - W)

        attend(sin_a.at[0], sin_a.at[1], NSINK // TQ, [sink_mask(i) for i in range(NSINK // TQ)])

    for g in range(G):
        r = pl.ds(g * TQ, TQ)
        total = jnp.sum(l_ref[r], axis=1, keepdims=True)
        o_ref[:, g * HD : (g + 1) * HD] = (acc[r] / total).astype(BF)

    for kv in range(2):
        for j, shift, there in sends:
            copy(kv, j, shift, there).wait_send()

    @pl.when(y == 0)
    def _():
        sink_copy(sin_a, 0, 32).wait_send()
        sink_copy(sin_a, 1, 48).wait_send()

    @pl.when(y == 1)
    def _():
        sink_copy(sin_b, 2, 32).wait_send()


def local(queries, hidden, key_value_weight, key_value_bias, positions, sink_index):
    vmem = pl.BlockSpec(memory_space=pltpu.VMEM)
    dma = pltpu.SemaphoreType.DMA
    flops = 2 * 512 * 512 * DL
    q_rot, k_own, v_own = pl.pallas_call(
        project,
        out_shape=[
            jax.ShapeDtypeStruct((G * TQ, HD), BF),
            jax.ShapeDtypeStruct((TQ, HD), BF),
            jax.ShapeDtypeStruct((TQ, HD), BF),
        ],
        in_specs=[vmem] * 5,
        out_specs=[vmem] * 3,
        scratch_shapes=[
            pltpu.VMEM((NY, TQ, DL), BF),
            pltpu.VMEM((2, 2 * HD, DL), BF),
            pltpu.VMEM((NY, TQ, 2 * HD), F32),
            pltpu.VMEM((NY, TQ, 2 * HD), F32),
            pltpu.VMEM((NY, TQ, 2 * HD), F32),
            pltpu.VMEM((NX, TQ, 2 * HD), F32),
            pltpu.VMEM((TQ, HD), F32),
            pltpu.VMEM((TQ, HD), F32),
            dma((NY,)),
            dma((NY,)),
            dma((9, 2)),
            dma((9, 2)),
            dma((9, 2)),
            dma((9, 2)),
            dma((NY,)),
            dma((NY,)),
            dma((NX,)),
            dma((NX,)),
        ],
        compiler_params=pltpu.CompilerParams(
            collective_id=0, has_side_effects=True, vmem_limit_bytes=32 * 2**20
        ),
        cost_estimate=pl.CostEstimate(flops=flops, bytes_accessed=2**20, transcendentals=2**15),
        name="project",
    )(queries, hidden, jnp.swapaxes(key_value_weight, 1, 2), key_value_bias, positions)
    keys = W + TQ + NSINK
    return pl.pallas_call(
        attention,
        out_shape=jax.ShapeDtypeStruct((TQ, G * HD), BF),
        in_specs=[vmem] * 4,
        out_specs=vmem,
        scratch_shapes=[
            pltpu.VMEM((33 * TQ, HD), BF),
            pltpu.VMEM((33 * TQ, HD), BF),
            pltpu.VMEM((G * TQ, HD), F32),
            pltpu.VMEM((G * TQ, HD), F32),
            pltpu.VMEM((G * TQ, HD), F32),
            pltpu.VMEM((2, NSINK, HD), F32),
            pltpu.VMEM((2, NSINK, HD), BF),
            pltpu.VMEM((2, NSINK, HD), BF),
            pltpu.VMEM((2, NSINK, HD), BF),
            dma((2, 33)),
            dma((2, 33)),
            dma((3,)),
            dma((3,)),
        ],
        compiler_params=pltpu.CompilerParams(
            collective_id=1, has_side_effects=True, vmem_limit_bytes=32 * 2**20
        ),
        cost_estimate=pl.CostEstimate(
            flops=4 * G * TQ * keys * HD, bytes_accessed=2**20, transcendentals=G * TQ * keys
        ),
        name="attention",
    )(q_rot, k_own, v_own, sink_index.reshape(1, NSINK))


def solution(mesh):
    placed = (
        P("seq", "tensor"),
        P("seq", "tensor"),
        P(None, "tensor", "seq"),
        P(None, "tensor"),
        P(None, "seq"),
        P(),
    )
    return jax.shard_map(
        local, mesh=mesh, in_specs=placed, out_specs=P("seq", "tensor"), check_vma=False
    )
```

time: 693 us -> 139 us (0.20)
  the two profiles are of different devices: /device:TPU:96 before, /device:TPU:24 now
where the time goes in v1:
time: 139 us; the launch traced here: 138 us
  Pallas kernels  133 us (96%)
  local copies, waits for them, and re-layouts  4.8 us (3%)
    pallas_call x1, Pallas kernels, local(): pl.pallas_call(project, out_shape=[jax.ShapeDtypeStruct((G * TQ, HD), BF)...  67.4 us
    pallas_call x1, Pallas kernels, local(): pl.pallas_call(attention, out_shape=jax.ShapeDtypeStruct((TQ, G * HD), BF...  65.8 us
    unnamed x13, local copies, waits for them, and re-layouts  4.8 us

profile of v1, /device:TPU:24, one launch (start us, length us, event | category | flops | bytes accessed | tf_op | source)
XLA Modules:
  0.0 138.1 jit_solution(12178389103934495944)
XLA Ops:
  0.0 0.0 copy-start.3
  0.0 0.0 copy-start.5
  0.0 0.7 copy-done.3
  0.7 0.0 copy-done.5
  0.7 0.0 copy-start
  0.7 0.9 copy-done
  1.6 0.0 copy-start.1
  1.6 0.9 copy-done.1
  2.6 0.0 copy-start.2
  2.6 0.8 copy-done.2
  3.4 67.4 %project.1 = (bf16[1024,128]{1,0:T(8,128)(2,1)S(1)}, bf16[128,128]{1,0:T(8,128)(2,1)S(1)}, bf16[128,128]{1,0:T(8,128)(2,1)S(1)}) custom-call(bf16[128,1024]{1,0:T(8,128)(2,1)S(1)} %copy-done, bf16[128,1024]{1,0:T(8,128)(2,1)S(1)} %copy-done.1, bf16[2,16,1024]{2,1,0:T(8,128)(2,1)S(1)} %bitcast.2, bf16[2,128]{1,0:T(2,128)(2,1)S(1)} %copy-done.5, ...), custom_call_target="tpu_custom_call" | custom-call | flops 536870912 | bytes 1048576 | tf_op jit(solution)/shard_map/project/pallas_call | solution.py:418
  70.9 0.0 copy-start.4
  70.9 0.7 copy-done.4
  71.6 65.8 %attention.1 = bf16[128,1024]{1,0:T(8,128)(2,1)S(1)} custom-call(bf16[1024,128]{1,0:T(8,128)(2,1)S(1)} %get-tuple-element.8.q_ref, bf16[128,128]{1,0:T(8,128)(2,1)S(1)} %get-tuple-element.9.k_ref, bf16[128,128]{1,0:T(8,128)(2,1)S(1)} %get-tuple-element.10.v_ref, s32[1,512]{1,0:T(1,128)S(1)} %bitcast.3), custom_call_target="tpu_custom_call" | custom-call | flops 2483027968 | bytes 1048576 | tf_op jit(solution)/shard_map/attention/pallas_call | solution.py:454
  137.4 0.7 copy.8
Async XLA Ops:
  0.0 0.7 copy-start.3
  0.0 0.7 copy-start.5
  0.7 1.0 copy-start
  1.6 0.9 copy-start.1
  2.6 0.8 copy-start.2
  70.9 0.7 copy-start.4

commit v2 on v0

v2 whole, which is shorter than its diff:
```python
import functools
import math

import jax
import jax.numpy as jnp
from jax import lax
from jax.experimental import pallas as pl
from jax.experimental.pallas import tpu as pltpu
from jax.sharding import PartitionSpec as P

H = 64
KVH = 8
HD = 128
W = 4096
NX = 4
NY = 4
NZ = 16
NS = NY * NZ
TQ = 128
G = H // KVH
DL = 1024
NSINK = 512
MESH = pl.DeviceIdType.MESH
LOG2E = 1.4426950408889634
BF = jnp.bfloat16
F32 = jnp.float32


def coords():
    s = lax.axis_index("seq")
    t = lax.axis_index("tensor")
    return s, t, t // 2, t % 2, s // NZ, s % NZ


def remote(src, dst, send, recv, seq, tensor):
    return pltpu.make_async_remote_copy(
        src_ref=src,
        dst_ref=dst,
        send_sem=send,
        recv_sem=recv,
        device_id=(seq, tensor),
        device_id_type=MESH,
    )


def nt_dot(a, b):
    return lax.dot_general(a, b, (((1,), (1,)), ((), ())), preferred_element_type=F32)


def rope_tables(pos):
    half = HD // 2
    pair = lax.broadcasted_iota(jnp.int32, (half, TQ), 0)
    inverse = jnp.exp(pair.astype(F32) * (-2.0 * math.log(1000000.0) / HD))
    first = HD // 8
    second = first + 3 * HD // 16
    temporal, height, width = (jnp.broadcast_to(pos[i : i + 1], (half, TQ)) for i in range(3))
    chosen = jnp.where(pair < first, temporal, jnp.where(pair < second, height, width))
    angles = chosen * inverse
    return jnp.cos(angles), jnp.sin(angles)


def rotate(u, tables):
    cosine, sine = tables
    top, low = u[: HD // 2], u[HD // 2 :]
    return jnp.concatenate([top * cosine - low * sine, low * cosine + top * sine], axis=0)


W_ONWARD = {
    0: [1, -1, 2, -2],
    1: [2], 2: [2], 3: [2], 4: [2], 5: [2], 6: [2],
    15: [-2], 14: [-2], 13: [-2], 12: [-2], 11: [-2],
}
W_ROUNDS = [[1, 15, 2, 14], [3, 13, 4, 12], [5, 11, 6, 10], [7, 9, 8]]


def project(
    q_ref, h_ref, w_ref, b_ref, p_ref, qo_ref, kv_ref,
    hid, wbuf, p3s, p3r, p4s, p4r, pos, bias, kvs, kvr,
    hs, hr, ws, wr, p3ss, p3rs, p4ss, p4rs, ps, pr, ts, tr,
):
    s, t, x, c, y, z = coords()
    other = x * 2 + (1 - c)
    mine = x == y

    def on_z(d):
        return y * NZ + lax.rem(z + d + NZ, NZ)

    def on_y(d):
        return lax.rem(y + d, NY) * NZ + z

    def on_x(d):
        return lax.rem(x + d, NX) * 2 + c

    barrier = pltpu.get_barrier_semaphore()

    def greet(seq, tensor):
        pl.semaphore_signal(barrier, inc=1, device_id=(seq, tensor), device_id_type=MESH)

    greet(s, other)
    for d in (1, -1, 2, -2):
        greet(on_z(d), t)
    for d in range(1, NY):
        greet(on_y(d), t)
        greet(s, on_x(d))

    @pl.when(jnp.logical_not(mine))
    def _():
        greet(x * NZ + z, y * 2 + c)

    wbuf[z // 8, lax.rem(z, 8)] = w_ref[...]
    hid[y] = h_ref[...]
    pos[0:3] = p_ref[...].astype(F32)
    pos[3:8] = jnp.zeros((5, TQ), F32)
    own_tables = rope_tables(pos[0:8])
    bias[0:2] = b_ref[...].astype(F32)
    bias[2:8] = jnp.zeros((6, HD), F32)
    pl.semaphore_wait(barrier, jnp.where(mine, 11, 12))

    def w_block(d):
        origin = lax.rem(z - d + NZ, NZ)
        return wbuf.at[origin // 8, lax.rem(origin, 8)]

    def w_copy(kv, d, hop):
        there = (d + hop) % NZ
        block = w_block(d).at[kv]
        return remote(block, block, ws.at[kv, there], wr.at[kv, there], on_z(hop), t)

    def w_forward(kv, d):
        for hop in W_ONWARD.get(d, []):
            w_copy(kv, d, hop).start()

    def w_wait(kv, d):
        block = w_block(d).at[kv]
        remote(block, block, ws.at[kv, d], wr.at[kv, d], s, t).wait_recv()

    for kv in range(2):
        w_forward(kv, 0)

    def h_copy(d):
        return remote(h_ref, hid.at[y], hs.at[d], hr.at[d], on_y(d), t)

    for d in (1, 3, 2):
        h_copy(d).start()

    def p_copy(d):
        return remote(pos.at[pl.ds(0, 8)], pos.at[pl.ds(8, 8)], ps.at[0, d], pr.at[0], on_y(d), t)

    def b_copy(d):
        return remote(bias.at[pl.ds(0, 8)], bias.at[pl.ds(8, 8)], ps.at[1, d], pr.at[1], s, on_x(d))

    @pl.when(mine)
    def _():
        pos[8:16] = pos[0:8]
        bias[8:16] = bias[0:8]
        for d in range(1, NY):
            p_copy(d).start()
            b_copy(d).start()

    def turn_query(g):
        u = jnp.transpose(q_ref[:, g * HD : (g + 1) * HD].astype(F32))
        qo_ref[:, g * TQ : (g + 1) * TQ] = rotate(u, own_tables).astype(BF)

    for index, arrived in enumerate(W_ROUNDS):
        for kv in range(2):
            for d in arrived:
                w_wait(kv, d)
                w_forward(kv, d)
        share = -(-G // (len(W_ROUNDS) - 1))
        for g in range(index * share, min((index + 1) * share, G)):
            turn_query(g)

    @pl.when(jnp.logical_not(mine))
    def _():
        p_copy(1).wait_recv()
        b_copy(1).wait_recv()

    tables = rope_tables(pos[8:16])
    for d in range(1, NY):
        slot = hid.at[lax.rem(y + NY - d, NY)]
        remote(slot, slot, hs.at[d], hr.at[d], s, t).wait_recv()

    def product(head, out):
        rows = hid[...].reshape(NY * TQ, DL)
        for kv in range(2):
            cols = wbuf[head, :, kv].reshape(HD, DL)
            part = nt_dot(rows, cols).reshape(NY, TQ, HD)
            for i in range(NY):
                out[i, kv] = part[i]

    def p3_copy(i):
        return remote(p3s.at[i], p3r.at[i], p3ss.at[i], p3rs.at[i], s, other)

    product(1 - c, p3s)
    for i in range(NY):
        p3_copy(i).start()
    product(c, p4s)

    def p4_copy(i):
        return remote(p4s.at[i], p4r.at[x], p4ss.at[i], p4rs.at[x], s, i * 2 + c)

    for i in range(NY):
        p3_copy(i).wait_recv()
        p4s[i] += p3r[i]

        @pl.when(x == i)
        def _(i=i):
            p4r[x] = p4s[i]

        @pl.when(x != i)
        def _(i=i):
            p4_copy(i).start()

    for i in range(NX):
        @pl.when(x != i)
        def _(i=i):
            remote(p4r.at[i], p4r.at[i], p4ss.at[i], p4rs.at[i], s, t).wait_recv()

    keys = (p4r[0, 0] + p4r[1, 0]) + (p4r[2, 0] + p4r[3, 0]) + bias[8:9]
    kvs[0] = jnp.transpose(rotate(jnp.transpose(keys), tables)).astype(BF)
    vals = (p4r[0, 1] + p4r[1, 1]) + (p4r[2, 1] + p4r[3, 1]) + bias[9:10]
    kvs[1] = jnp.transpose(vals).astype(BF)

    def t_copy():
        return remote(kvs, kvr, ts, tr, x * NZ + z, y * 2 + c)

    @pl.when(mine)
    def _():
        kv_ref[...] = kvs[...]

    @pl.when(jnp.logical_not(mine))
    def _():
        t_copy().start()
        t_copy().wait_recv()
        kv_ref[...] = kvr[...]

    for d, hops in W_ONWARD.items():
        for hop in hops:
            for kv in range(2):
                w_copy(kv, d, hop).wait_send()
    for d in range(1, NY):
        h_copy(d).wait_send()
    for i in range(NY):
        p3_copy(i).wait_send()

        @pl.when(x != i)
        def _(i=i):
            p4_copy(i).wait_send()

    @pl.when(mine)
    def _():
        for d in range(1, NY):
            p_copy(d).wait_send()
            b_copy(d).wait_send()

    @pl.when(jnp.logical_not(mine))
    def _():
        t_copy().wait_send()


ONWARD = {
    0: [(1, 1), (16, 16), (32, 32)],
    16: [(-1, 15)],
    32: [(-1, 31)],
    1: [(1, 2), (16, 17)],
    2: [(1, 3), (16, 18)],
    3: [(1, 4), (16, 19)],
    4: [(1, 5), (16, 20)],
    5: [(1, 6), (16, 21)],
    6: [(1, 7), (16, 22)],
    7: [(1, 8), (16, 23)],
    8: [(16, 24)],
    15: [(-1, 14)],
    14: [(-1, 13)],
    13: [(-1, 12)],
    12: [(-1, 11)],
    11: [(-1, 10)],
    10: [(-1, 9)],
    31: [(-1, 30)],
    30: [(-1, 29)],
    29: [(-1, 28)],
    28: [(-1, 27)],
    27: [(-1, 26)],
    26: [(-1, 25)],
}
ROUNDS = [
    ([1, 16], [1, 16]),
    ([2, 15, 32], [2, 15]),
    ([3, 14, 31], [3, 14]),
    ([17], [17, 31]),
    ([4, 13, 30], [4, 13]),
    ([18], [18, 30]),
    ([5, 12, 29], [5, 12]),
    ([19], [19, 29]),
    ([6, 11, 28], [6, 11]),
    ([20], [20, 28]),
    ([7, 10, 27], [7, 10]),
    ([21], [21, 27]),
    ([8, 9, 26], [8, 9]),
    ([22], [22, 26]),
    ([25, 23, 24], [23, 24, 25, 32]),
]
SINKS_AFTER = 12
SLOT = {0: 0}
for _, group in ROUNDS:
    for j in group:
        SLOT[j] = len(SLOT)


def attention(
    q_ref, kv_ref, i_ref, o_ref,
    buf, acc, m_ref, l_ref, column, sacc_k, sacc_v, out_k, out_v, in_k, in_v, more_k, more_v, cs, cr, ss, sr,
):
    s, t, x, c, y, z = coords()

    def at(shift):
        return lax.rem(s + shift + NS, NS)

    barrier = pltpu.get_barrier_semaphore()
    for shift in (1, -1, 2, -2, 16, -16, 32):
        pl.semaphore_signal(barrier, inc=1, device_id=(at(shift), t), device_id_type=MESH)
    buf[0] = kv_ref[...]
    pl.semaphore_wait(barrier, 7)

    def copy(kv, j, shift, there):
        src, dst = buf.at[SLOT[j], kv], buf.at[SLOT[there], kv]
        return remote(src, dst, cs.at[kv, there], cr.at[kv, there], at(shift), t)

    def forward(kv, j):
        for shift, there in ONWARD.get(j, []):
            copy(kv, j, shift, there).start()

    for kv in range(2):
        forward(kv, 0)

    sink_row = i_ref[...]
    for i in range(NSINK // TQ):
        part = jnp.broadcast_to(sink_row[:, i * TQ : (i + 1) * TQ], (TQ, TQ)).astype(F32)
        column[i] = jnp.transpose(part)

    scale = HD ** (-0.5)
    k_row = lax.broadcasted_iota(jnp.int32, (TQ, TQ), 0)
    q_col = lax.broadcasted_iota(jnp.int32, (TQ, TQ), 1)

    def attend(keys, values, masks, first=False):
        n = len(masks)
        for g in range(G):
            cols = slice(g * TQ, (g + 1) * TQ)
            scores = jnp.dot(keys(), q_ref[:, cols], preferred_element_type=F32)
            tiles = []
            for i, mask in enumerate(masks):
                tile = scores[i * TQ : (i + 1) * TQ]
                tiles.append(tile if mask is None else jnp.where(mask(), tile, -1e30))
            scores = jnp.concatenate(tiles, axis=0).reshape(n * TQ // 8, 8, TQ)
            top = jnp.max(jnp.max(scores, axis=0), axis=0, keepdims=True) * scale
            top = jnp.broadcast_to(top, (8, TQ))
            if not first:
                old = m_ref[:, cols]
                top = jnp.maximum(old, top)
                factor = jnp.exp(old - top)
            m_ref[:, cols] = top
            weights = jnp.exp(scores * scale - top[None])
            summed = jnp.sum(weights, axis=0)
            out = jnp.dot(values(), weights.reshape(n * TQ, TQ).astype(BF), preferred_element_type=F32)
            if first:
                l_ref[:, cols] = summed
                acc[:, cols] = out
            else:
                l_ref[:, cols] = l_ref[:, cols] * factor + summed
                scaled = acc[:, cols].reshape(HD // 8, 8, TQ) * factor[None]
                acc[:, cols] = scaled.reshape(HD, TQ) + out

    def attend_blocks(group, masks, first=False):
        start, n = SLOT[group[0]], len(group)
        attend(
            lambda: buf[start : start + n, 0].reshape(n * TQ, HD),
            lambda: jnp.concatenate([buf[start + i, 1] for i in range(n)], axis=1),
            masks,
            first,
        )

    def mask_of(j, guard):
        if j == 32:
            return lambda: (k_row > q_col) & (s >= 32)
        return (lambda: jnp.broadcast_to(s >= j, (TQ, TQ))) if guard else None

    def group_attend(group):
        @pl.when(s >= max(group))
        def _():
            attend_blocks(group, [mask_of(j, False) for j in group])

        @pl.when((s >= min(group)) & (s < max(group)))
        def _():
            attend_blocks(group, [mask_of(j, True) for j in group])

    def extract(j):
        base = (s - j) * TQ
        token = (q_col + base).astype(F32)
        hot = jnp.concatenate(
            [jnp.where(column[i] == token, 1.0, 0.0).astype(BF) for i in range(NSINK // TQ)], axis=0
        )
        k_part = jnp.dot(hot, buf[SLOT[j], 0], preferred_element_type=F32)
        across = jnp.broadcast_to(sink_row, (TQ, NSINK)) - base
        hot = jnp.where(across == lax.broadcasted_iota(jnp.int32, (TQ, NSINK), 0), 1.0, 0.0).astype(BF)
        v_part = jnp.dot(buf[SLOT[j], 1], hot, preferred_element_type=F32)
        if j == 0:
            sacc_k[...] = k_part
            sacc_v[...] = v_part
        else:
            sacc_k[...] += k_part
            sacc_v[...] += v_part

    attend_blocks([0], [lambda: k_row <= q_col], first=True)

    @pl.when(y < 2)
    def _():
        extract(0)

    def sink_copies(more, n, shift):
        dst_k, dst_v = (more_k, more_v) if more else (in_k, in_v)
        return (
            remote(out_k, dst_k, ss.at[n, 0], sr.at[n, 0], at(shift), t),
            remote(out_v, dst_v, ss.at[n, 1], sr.at[n, 1], at(shift), t),
        )

    for index, (waits, group) in enumerate(ROUNDS):
        for kv in range(2):
            for j in waits:
                copy(kv, j, 1, j).wait_recv()
                forward(kv, j)
        group_attend(group)
        for j in group:
            if j < 16:
                @pl.when((y < 2) & (s >= j))
                def _(j=j):
                    extract(j)
        if index == SINKS_AFTER:
            @pl.when(y < 2)
            def _():
                out_k[...] = sacc_k[...].astype(BF)
                out_v[...] = sacc_v[...].astype(BF)

            @pl.when(y == 0)
            def _():
                for one in sink_copies(False, 1, 48) + sink_copies(False, 0, 32):
                    one.start()

            @pl.when(y == 1)
            def _():
                for one in sink_copies(True, 2, 32):
                    one.start()

    @pl.when(y == 2)
    def _():
        for one in sink_copies(False, 0, 32):
            one.wait_recv()

    @pl.when(y == 3)
    def _():
        for one in sink_copies(False, 1, 48) + sink_copies(True, 2, 32):
            one.wait_recv()
        in_k[...] = in_k[...] + more_k[...]
        in_v[...] = in_v[...] + more_v[...]

    @pl.when(y >= 2)
    def _():
        limit = (q_col + (s * TQ - W)).astype(F32)
        attend(
            lambda: in_k[...],
            lambda: in_v[...],
            [lambda i=i: column[i] <= limit for i in range(NSINK // TQ)],
        )

    for g in range(G):
        cols = slice(g * TQ, (g + 1) * TQ)
        total = jnp.sum(l_ref[:, cols], axis=0, keepdims=True)
        o_ref[:, cols] = jnp.transpose(acc[:, cols] / total).astype(BF)

    for j, moves in ONWARD.items():
        for shift, there in moves:
            for kv in range(2):
                copy(kv, j, shift, there).wait_send()

    @pl.when(y == 0)
    def _():
        for one in sink_copies(False, 1, 48) + sink_copies(False, 0, 32):
            one.wait_send()

    @pl.when(y == 1)
    def _():
        for one in sink_copies(True, 2, 32):
            one.wait_send()


def local(queries, hidden, key_value_weight, key_value_bias, positions, sink_index):
    vmem = pl.BlockSpec(memory_space=pltpu.VMEM)
    dma = pltpu.SemaphoreType.DMA
    flops = 2 * 512 * 512 * DL
    q_turned, own = pl.pallas_call(
        project,
        out_shape=[
            jax.ShapeDtypeStruct((HD, G * TQ), BF),
            jax.ShapeDtypeStruct((2, TQ, HD), BF),
        ],
        in_specs=[vmem] * 5,
        out_specs=[vmem] * 2,
        scratch_shapes=[
            pltpu.VMEM((NY, TQ, DL), BF),
            pltpu.VMEM((2, 8, 2, 16, DL), BF),
            pltpu.VMEM((NY, 2, TQ, HD), F32),
            pltpu.VMEM((NY, 2, TQ, HD), F32),
            pltpu.VMEM((NY, 2, TQ, HD), F32),
            pltpu.VMEM((NX, 2, TQ, HD), F32),
            pltpu.VMEM((16, TQ), F32),
            pltpu.VMEM((16, HD), F32),
            pltpu.VMEM((2, TQ, HD), BF),
            pltpu.VMEM((2, TQ, HD), BF),
            dma((NY,)),
            dma((NY,)),
            dma((2, NZ)),
            dma((2, NZ)),
            dma((NY,)),
            dma((NY,)),
            dma((NX,)),
            dma((NX,)),
            dma((2, NY)),
            dma((2,)),
            dma,
            dma,
        ],
        compiler_params=pltpu.CompilerParams(
            collective_id=0, has_side_effects=True, vmem_limit_bytes=32 * 2**20
        ),
        cost_estimate=pl.CostEstimate(flops=flops, bytes_accessed=2**20, transcendentals=2**15),
        name="project",
    )(queries, hidden, jnp.swapaxes(key_value_weight, 1, 2), key_value_bias, positions)
    keys = W + TQ + NSINK
    return pl.pallas_call(
        attention,
        out_shape=jax.ShapeDtypeStruct((TQ, G * HD), BF),
        in_specs=[vmem] * 3,
        out_specs=vmem,
        scratch_shapes=[
            pltpu.VMEM((33, 2, TQ, HD), BF),
            pltpu.VMEM((HD, G * TQ), F32),
            pltpu.VMEM((8, G * TQ), F32),
            pltpu.VMEM((8, G * TQ), F32),
            pltpu.VMEM((NSINK // TQ, TQ, TQ), F32),
            pltpu.VMEM((NSINK, HD), F32),
            pltpu.VMEM((HD, NSINK), F32),
        ]
        + [pltpu.VMEM((NSINK, HD), BF), pltpu.VMEM((HD, NSINK), BF)] * 3
        + [dma((2, 33)), dma((2, 33)), dma((3, 2)), dma((3, 2))],
        compiler_params=pltpu.CompilerParams(
            collective_id=1, has_side_effects=True, vmem_limit_bytes=32 * 2**20
        ),
        cost_estimate=pl.CostEstimate(
            flops=4 * G * TQ * keys * HD, bytes_accessed=2**20, transcendentals=G * TQ * keys
        ),
        name="attention",
    )(q_turned, own, sink_index.reshape(1, NSINK))


def solution(mesh):
    placed = (
        P("seq", "tensor"),
        P("seq", "tensor"),
        P(None, "tensor", "seq"),
        P(None, "tensor"),
        P(None, "seq"),
        P(),
    )
    return jax.shard_map(
        local, mesh=mesh, in_specs=placed, out_specs=P("seq", "tensor"), check_vma=False
    )
```

time: 693 us -> 108 us (0.16)
  the two profiles are of different devices: /device:TPU:96 before, /device:TPU:24 now
where the time goes in v2:
time: 108 us; the launch traced here: 107 us
  Pallas kernels  103 us (95%)
  local copies, waits for them, and re-layouts  4.8 us (4%)
    pallas_call x1, Pallas kernels, local(): pl.pallas_call(project, out_shape=[jax.ShapeDtypeStruct((HD, G * TQ), BF)...  53.9 us
    pallas_call x1, Pallas kernels, local(): pl.pallas_call(attention, out_shape=jax.ShapeDtypeStruct((TQ, G * HD), BF...  48.7 us
    unnamed x13, local copies, waits for them, and re-layouts  4.8 us

profile of v2, /device:TPU:24, one launch (start us, length us, event | category | flops | bytes accessed | tf_op | source)
XLA Modules:
  0.0 107.4 jit_solution(6704537248910881296)
XLA Ops:
  0.0 0.0 copy-start.3
  0.0 0.0 copy-start.5
  0.0 0.7 copy-done.3
  0.7 0.0 copy-done.5
  0.7 0.0 copy-start
  0.7 0.9 copy-done
  1.6 0.0 copy-start.1
  1.6 0.9 copy-done.1
  2.6 0.0 copy-start.2
  2.6 0.8 copy-done.2
  3.4 53.9 %project.1 = (bf16[128,1024]{1,0:T(8,128)(2,1)S(1)}, bf16[2,128,128]{2,1,0:T(8,128)(2,1)S(1)}) custom-call(bf16[128,1024]{1,0:T(8,128)(2,1)S(1)} %copy-done, bf16[128,1024]{1,0:T(8,128)(2,1)S(1)} %copy-done.1, bf16[2,16,1024]{2,1,0:T(8,128)(2,1)S(1)} %bitcast.2, bf16[2,128]{1,0:T(2,128)(2,1)S(1)} %copy-done.5, s32[3,128]{1,0:T(4,128)S(1)} %copy-done.3), custom_call_target="tpu_custom_call" | custom-call | flops 536870912 | bytes 1048576 | tf_op jit(solution)/shard_map/project/pallas_call | solution.py:498
  57.4 0.0 copy-start.4
  57.4 0.7 copy-done.4
  58.1 48.7 %attention.1 = bf16[128,1024]{1,0:T(8,128)(2,1)S(1)} custom-call(bf16[128,1024]{1,0:T(8,128)(2,1)S(1)} %get-tuple-element.7.q_ref, bf16[2,128,128]{2,1,0:T(8,128)(2,1)S(1)} %get-tuple-element.8.kv_ref, s32[1,512]{1,0:T(1,128)S(1)} %bitcast.3), custom_call_target="tpu_custom_call" | custom-call | flops 2483027968 | bytes 1048576 | tf_op jit(solution)/shard_map/attention/pallas_call | solution.py:537
  106.7 0.7 copy.8
Async XLA Ops:
  0.0 0.7 copy-start.3
  0.0 0.7 copy-start.5
  0.7 1.0 copy-start
  1.6 0.9 copy-start.1
  2.6 0.8 copy-start.2
  57.4 0.7 copy-start.4

commit v3 on v2

--- a/solution.py
+++ b/solution.py
@@ -74,9 +74,9 @@
 
 
 def project(
-    q_ref, h_ref, w_ref, b_ref, p_ref, qo_ref, kv_ref,
-    hid, wbuf, p3s, p3r, p4s, p4r, pos, bias, kvs, kvr,
-    hs, hr, ws, wr, p3ss, p3rs, p4ss, p4rs, ps, pr, ts, tr,
+    q_hbm, h_hbm, w_hbm, b_hbm, p_hbm, i_hbm, qo_ref, first_block, sinks,
+    q_ref, b_ref, p_ref, hid, wbuf, p3s, p3r, p4s, p4r, pos, bias, kvs,
+    ins, hs, hr, ws, wr, p3ss, p3rs, p4ss, p4rs, ps, pr, ts, tr,
 ):
     s, t, x, c, y, z = coords()
     other = x * 2 + (1 - c)
@@ -96,7 +96,18 @@
     def greet(seq, tensor):
         pl.semaphore_signal(barrier, inc=1, device_id=(seq, tensor), device_id_type=MESH)
 
+    own_w = wbuf.at[z // 8, lax.rem(z, 8)]
+    loads = [
+        pltpu.make_async_copy(src, dst, ins.at[i])
+        for i, (src, dst) in enumerate(
+            [(w_hbm, own_w), (h_hbm, hid.at[y]), (p_hbm, p_ref), (b_hbm, b_ref), (q_hbm, q_ref), (i_hbm, sinks)]
+        )
+    ]
+    for load in loads:
+        load.start()
     greet(s, other)
+    for d in (1, -1):
+        greet(lax.rem(s + d + NS, NS), t)
     for d in (1, -1, 2, -2):
         greet(on_z(d), t)
     for d in range(1, NY):
@@ -107,14 +118,8 @@
     def _():
         greet(x * NZ + z, y * 2 + c)
 
-    wbuf[z // 8, lax.rem(z, 8)] = w_ref[...]
-    hid[y] = h_ref[...]
-    pos[0:3] = p_ref[...].astype(F32)
-    pos[3:8] = jnp.zeros((5, TQ), F32)
-    own_tables = rope_tables(pos[0:8])
-    bias[0:2] = b_ref[...].astype(F32)
-    bias[2:8] = jnp.zeros((6, HD), F32)
-    pl.semaphore_wait(barrier, jnp.where(mine, 11, 12))
+    pl.semaphore_wait(barrier, jnp.where(mine, 13, 14))
+    loads[0].wait()
 
     def w_block(d):
         origin = lax.rem(z - d + NZ, NZ)
@@ -137,10 +142,17 @@
         w_forward(kv, 0)
 
     def h_copy(d):
-        return remote(h_ref, hid.at[y], hs.at[d], hr.at[d], on_y(d), t)
-
+        return remote(hid.at[y], hid.at[y], hs.at[d], hr.at[d], on_y(d), t)
+
+    loads[1].wait()
     for d in (1, 3, 2):
         h_copy(d).start()
+    for load in loads[2:]:
+        load.wait()
+    pos[0:3] = p_ref[...].astype(F32)
+    pos[3:8] = jnp.zeros((5, TQ), F32)
+    bias[0:2] = b_ref[...].astype(F32)
+    bias[2:8] = jnp.zeros((6, HD), F32)
 
     def p_copy(d):
         return remote(pos.at[pl.ds(0, 8)], pos.at[pl.ds(8, 8)], ps.at[0, d], pr.at[0], on_y(d), t)
@@ -155,6 +167,8 @@
         for d in range(1, NY):
             p_copy(d).start()
             b_copy(d).start()
+
+    own_tables = rope_tables(pos[0:8])
 
     def turn_query(g):
         u = jnp.transpose(q_ref[:, g * HD : (g + 1) * HD].astype(F32))
@@ -221,40 +235,42 @@
     kvs[1] = jnp.transpose(vals).astype(BF)
 
     def t_copy():
-        return remote(kvs, kvr, ts, tr, x * NZ + z, y * 2 + c)
+        return remote(kvs, first_block, ts, tr, x * NZ + z, y * 2 + c)
 
     @pl.when(mine)
     def _():
-        kv_ref[...] = kvs[...]
+        first_block[...] = kvs[...]
 
     @pl.when(jnp.logical_not(mine))
     def _():
         t_copy().start()
         t_copy().wait_recv()
-        kv_ref[...] = kvr[...]
-
-    for d, hops in W_ONWARD.items():
-        for hop in hops:
-            for kv in range(2):
-                w_copy(kv, d, hop).wait_send()
-    for d in range(1, NY):
-        h_copy(d).wait_send()
-    for i in range(NY):
-        p3_copy(i).wait_send()
-
-        @pl.when(x != i)
-        def _(i=i):
-            p4_copy(i).wait_send()
-
-    @pl.when(mine)
-    def _():
+
+    def finish():
+        for d, hops in W_ONWARD.items():
+            for hop in hops:
+                for kv in range(2):
+                    w_copy(kv, d, hop).wait_send()
         for d in range(1, NY):
-            p_copy(d).wait_send()
-            b_copy(d).wait_send()
-
-    @pl.when(jnp.logical_not(mine))
-    def _():
-        t_copy().wait_send()
+            h_copy(d).wait_send()
+        for i in range(NY):
+            p3_copy(i).wait_send()
+
+            @pl.when(x != i)
+            def _(i=i):
+                p4_copy(i).wait_send()
+
+        @pl.when(mine)
+        def _():
+            for d in range(1, NY):
+                p_copy(d).wait_send()
+                b_copy(d).wait_send()
+
+        @pl.when(jnp.logical_not(mine))
+        def _():
+            t_copy().wait_send()
+
+    return finish
 
 
 ONWARD = {
@@ -307,19 +323,13 @@
 
 
 def attention(
-    q_ref, kv_ref, i_ref, o_ref,
+    q_ref, i_ref, o_ref,
     buf, acc, m_ref, l_ref, column, sacc_k, sacc_v, out_k, out_v, in_k, in_v, more_k, more_v, cs, cr, ss, sr,
 ):
     s, t, x, c, y, z = coords()
 
     def at(shift):
         return lax.rem(s + shift + NS, NS)
-
-    barrier = pltpu.get_barrier_semaphore()
-    for shift in (1, -1, 2, -2, 16, -16, 32):
-        pl.semaphore_signal(barrier, inc=1, device_id=(at(shift), t), device_id_type=MESH)
-    buf[0] = kv_ref[...]
-    pl.semaphore_wait(barrier, 7)
 
     def copy(kv, j, shift, there):
         src, dst = buf.at[SLOT[j], kv], buf.at[SLOT[there], kv]
@@ -493,71 +503,82 @@
 
 def local(queries, hidden, key_value_weight, key_value_bias, positions, sink_index):
     vmem = pl.BlockSpec(memory_space=pltpu.VMEM)
+    hbm = pl.BlockSpec(memory_space=pl.ANY)
     dma = pltpu.SemaphoreType.DMA
-    flops = 2 * 512 * 512 * DL
-    q_turned, own = pl.pallas_call(
-        project,
-        out_shape=[
-            jax.ShapeDtypeStruct((HD, G * TQ), BF),
-            jax.ShapeDtypeStruct((2, TQ, HD), BF),
-        ],
-        in_specs=[vmem] * 5,
-        out_specs=[vmem] * 2,
-        scratch_shapes=[
-            pltpu.VMEM((NY, TQ, DL), BF),
-            pltpu.VMEM((2, 8, 2, 16, DL), BF),
-            pltpu.VMEM((NY, 2, TQ, HD), F32),
-            pltpu.VMEM((NY, 2, TQ, HD), F32),
-            pltpu.VMEM((NY, 2, TQ, HD), F32),
-            pltpu.VMEM((NX, 2, TQ, HD), F32),
-            pltpu.VMEM((16, TQ), F32),
-            pltpu.VMEM((16, HD), F32),
-            pltpu.VMEM((2, TQ, HD), BF),
-            pltpu.VMEM((2, TQ, HD), BF),
-            dma((NY,)),
-            dma((NY,)),
-            dma((2, NZ)),
-            dma((2, NZ)),
-            dma((NY,)),
-            dma((NY,)),
-            dma((NX,)),
-            dma((NX,)),
-            dma((2, NY)),
-            dma((2,)),
-            dma,
-            dma,
-        ],
+    keys = W + TQ + NSINK
+    shared = [
+        pltpu.VMEM((HD, G * TQ), BF),
+        pltpu.VMEM((33, 2, TQ, HD), BF),
+        pltpu.VMEM((1, NSINK), jnp.int32),
+    ]
+    projecting = [
+        pltpu.VMEM((TQ, G * HD), BF),
+        pltpu.VMEM((2, HD), BF),
+        pltpu.VMEM((3, TQ), jnp.int32),
+        pltpu.VMEM((NY, TQ, DL), BF),
+        pltpu.VMEM((2, 8, 2, 16, DL), BF),
+        pltpu.VMEM((NY, 2, TQ, HD), F32),
+        pltpu.VMEM((NY, 2, TQ, HD), F32),
+        pltpu.VMEM((NY, 2, TQ, HD), F32),
+        pltpu.VMEM((NX, 2, TQ, HD), F32),
+        pltpu.VMEM((16, TQ), F32),
+        pltpu.VMEM((16, HD), F32),
+        pltpu.VMEM((2, TQ, HD), BF),
+        dma((6,)),
+        dma((NY,)),
+        dma((NY,)),
+        dma((2, NZ)),
+        dma((2, NZ)),
+        dma((NY,)),
+        dma((NY,)),
+        dma((NX,)),
+        dma((NX,)),
+        dma((2, NY)),
+        dma((2,)),
+        dma,
+        dma,
+    ]
+    attending = [
+        pltpu.VMEM((HD, G * TQ), F32),
+        pltpu.VMEM((8, G * TQ), F32),
+        pltpu.VMEM((8, G * TQ), F32),
+        pltpu.VMEM((NSINK // TQ, TQ, TQ), F32),
+        pltpu.VMEM((NSINK, HD), F32),
+        pltpu.VMEM((HD, NSINK), F32),
+    ]
+    attending += [pltpu.VMEM((NSINK, HD), BF), pltpu.VMEM((HD, NSINK), BF)] * 3
+    attending += [dma((2, 33)), dma((2, 33)), dma((3, 2)), dma((3, 2))]
+
+    def whole(*refs):
+        inputs, o_ref, refs = refs[:6], refs[6], refs[7:]
+        (turned, buf, sinks), refs = refs[:3], refs[3:]
+        finish = project(*inputs, turned, buf.at[0], sinks, *refs[: len(projecting)])
+        attention(turned, sinks, o_ref, buf, *refs[len(projecting) :])
+        finish()
+
+    return pl.pallas_call(
+        whole,
+        out_shape=jax.ShapeDtypeStruct((TQ, G * HD), BF),
+        in_specs=[hbm] * 6,
+        out_specs=vmem,
+        scratch_shapes=shared + projecting + attending,
         compiler_params=pltpu.CompilerParams(
-            collective_id=0, has_side_effects=True, vmem_limit_bytes=32 * 2**20
-        ),
-        cost_estimate=pl.CostEstimate(flops=flops, bytes_accessed=2**20, transcendentals=2**15),
-        name="project",
-    )(queries, hidden, jnp.swapaxes(key_value_weight, 1, 2), key_value_bias, positions)
-    keys = W + TQ + NSINK
-    return pl.pallas_call(
-        attention,
-        out_shape=jax.ShapeDtypeStruct((TQ, G * HD), BF),
-        in_specs=[vmem] * 3,
-        out_specs=vmem,
-        scratch_shapes=[
-            pltpu.VMEM((33, 2, TQ, HD), BF),
-            pltpu.VMEM((HD, G * TQ), F32),
-            pltpu.VMEM((8, G * TQ), F32),
-            pltpu.VMEM((8, G * TQ), F32),
-            pltpu.VMEM((NSINK // TQ, TQ, TQ), F32),
-            pltpu.VMEM((NSINK, HD), F32),
-            pltpu.VMEM((HD, NSINK), F32),
-        ]
-        + [pltpu.VMEM((NSINK, HD), BF), pltpu.VMEM((HD, NSINK), BF)] * 3
-        + [dma((2, 33)), dma((2, 33)), dma((3, 2)), dma((3, 2))],
-        compiler_params=pltpu.CompilerParams(
-            collective_id=1, has_side_effects=True, vmem_limit_bytes=32 * 2**20
+            collective_id=0, has_side_effects=True, vmem_limit_bytes=56 * 2**20
         ),
         cost_estimate=pl.CostEstimate(
-            flops=4 * G * TQ * keys * HD, bytes_accessed=2**20, transcendentals=G * TQ * keys
+            flops=4 * G * TQ * keys * HD + 2 * 512 * 512 * DL,
+            bytes_accessed=2**20,
+            transcendentals=G * TQ * keys,
         ),
-        name="attention",
-    )(q_turned, own, sink_index.reshape(1, NSINK))
+        name="windowed",
+    )(
+        queries,
+        hidden,
+        jnp.swapaxes(key_value_weight, 1, 2),
+        key_value_bias,
+        positions,
+        sink_index.reshape(1, NSINK),
+    )
 
 
 def solution(mesh):

time: 108 us -> 102 us (0.944)
  local copies, waits for them, and re-layouts: 4.8 us -> 1.67 us
  Pallas kernels: 103 us -> 100 us
    unnamed x13 -> x1, local copies, waits for them, and re-layouts: 4.8 us -> 1.67 us
    pallas_call x2 -> x1, Pallas kernels: 103 us -> 100 us  [local(): pl.pallas_call(whole, out_shape=jax.ShapeDtypeStruct((TQ, G * HD), BF), i...]
where the time goes in v3:
time: 102 us
  Pallas kernels  100 us (98%)
  local copies, waits for them, and re-layouts  1.67 us (2%)
    pallas_call x1, Pallas kernels, local(): pl.pallas_call(whole, out_shape=jax.ShapeDtypeStruct((TQ, G * HD), BF), i...  100 us

profile of v3, /device:TPU:24, one launch (start us, length us, event | category | flops | bytes accessed | tf_op | source)
XLA Modules:
  0.0 101.7 jit_solution(13893027687494654765)
XLA Ops:
  0.0 100.0 %windowed.1 = bf16[128,1024]{1,0:T(8,128)(2,1)} custom-call(bf16[128,1024]{1,0:T(8,128)(2,1)} %refs_0_.1, bf16[128,1024]{1,0:T(8,128)(2,1)} %refs_1_.1, bf16[2,16,1024]{2,1,0:T(8,128)(2,1)} %bitcast.2, bf16[2,128]{1,0:T(2,128)(2,1)} %refs_3_.1, s32[3,128]{1,0:T(4,128)} %refs_4_.1, s32[1,512]{1,0:T(1,128)} %bitcast.3), custom_call_target="tpu_custom_call" | custom-call | flops 3019898880 | bytes 1048576 | tf_op jit(solution)/shard_map/windowed/pallas_call | solution.py:559
  100.0 1.7 %copy.8 = bf16[128,1024]{1,0:T(8,128)(2,1)} copy(bf16[128,1024]{1,0:T(8,128)(2,1)} %windowed.1) | data formatting | bytes 524288

commit v4 on v3

--- a/solution.py
+++ b/solution.py
@@ -74,7 +74,7 @@
 
 
 def project(
-    q_hbm, h_hbm, w_hbm, b_hbm, p_hbm, i_hbm, qo_ref, first_block, sinks,
+    forward, q_hbm, h_hbm, w_hbm, b_hbm, p_hbm, i_hbm, qo_ref, first_block, sinks,
     q_ref, b_ref, p_ref, hid, wbuf, p3s, p3r, p4s, p4r, pos, bias, kvs,
     ins, hs, hr, ws, wr, p3ss, p3rs, p4ss, p4rs, ps, pr, ts, tr,
 ):
@@ -106,8 +106,8 @@
     for load in loads:
         load.start()
     greet(s, other)
-    for d in (1, -1):
-        greet(lax.rem(s + d + NS, NS), t)
+    for shift in SHIFTS:
+        greet(lax.rem(s - shift + NS, NS), t)
     for d in (1, -1, 2, -2):
         greet(on_z(d), t)
     for d in range(1, NY):
@@ -118,7 +118,7 @@
     def _():
         greet(x * NZ + z, y * 2 + c)
 
-    pl.semaphore_wait(barrier, jnp.where(mine, 13, 14))
+    pl.semaphore_wait(barrier, jnp.where(mine, 11, 12) + len(SHIFTS))
     loads[0].wait()
 
     def w_block(d):
@@ -174,7 +174,7 @@
         u = jnp.transpose(q_ref[:, g * HD : (g + 1) * HD].astype(F32))
         qo_ref[:, g * TQ : (g + 1) * TQ] = rotate(u, own_tables).astype(BF)
 
-    for index, arrived in enumerate(W_ROUNDS):
+    for index, arrived in enumerate(W_ROUNDS[:-1]):
         for kv in range(2):
             for d in arrived:
                 w_wait(kv, d)
@@ -193,58 +193,70 @@
         slot = hid.at[lax.rem(y + NY - d, NY)]
         remote(slot, slot, hs.at[d], hr.at[d], s, t).wait_recv()
 
-    def product(head, out):
+    def product(kv, head, out):
         rows = hid[...].reshape(NY * TQ, DL)
-        for kv in range(2):
-            cols = wbuf[head, :, kv].reshape(HD, DL)
-            part = nt_dot(rows, cols).reshape(NY, TQ, HD)
-            for i in range(NY):
-                out[i, kv] = part[i]
-
-    def p3_copy(i):
-        return remote(p3s.at[i], p3r.at[i], p3ss.at[i], p3rs.at[i], s, other)
-
-    product(1 - c, p3s)
-    for i in range(NY):
-        p3_copy(i).start()
-    product(c, p4s)
-
-    def p4_copy(i):
-        return remote(p4s.at[i], p4r.at[x], p4ss.at[i], p4rs.at[x], s, i * 2 + c)
-
-    for i in range(NY):
-        p3_copy(i).wait_recv()
-        p4s[i] += p3r[i]
-
-        @pl.when(x == i)
-        def _(i=i):
-            p4r[x] = p4s[i]
-
-        @pl.when(x != i)
-        def _(i=i):
-            p4_copy(i).start()
-
-    for i in range(NX):
-        @pl.when(x != i)
-        def _(i=i):
-            remote(p4r.at[i], p4r.at[i], p4ss.at[i], p4rs.at[i], s, t).wait_recv()
-
-    keys = (p4r[0, 0] + p4r[1, 0]) + (p4r[2, 0] + p4r[3, 0]) + bias[8:9]
-    kvs[0] = jnp.transpose(rotate(jnp.transpose(keys), tables)).astype(BF)
-    vals = (p4r[0, 1] + p4r[1, 1]) + (p4r[2, 1] + p4r[3, 1]) + bias[9:10]
-    kvs[1] = jnp.transpose(vals).astype(BF)
-
-    def t_copy():
-        return remote(kvs, first_block, ts, tr, x * NZ + z, y * 2 + c)
-
-    @pl.when(mine)
-    def _():
-        first_block[...] = kvs[...]
-
-    @pl.when(jnp.logical_not(mine))
-    def _():
-        t_copy().start()
-        t_copy().wait_recv()
+        cols = wbuf[head, :, kv].reshape(HD, DL)
+        part = nt_dot(rows, cols).reshape(NY, TQ, HD)
+        for i in range(NY):
+            out[kv, i] = part[i]
+
+    def p3_copy(kv, i):
+        return remote(p3s.at[kv, i], p3r.at[kv, i], p3ss.at[kv, i], p3rs.at[kv, i], s, other)
+
+    def p4_copy(kv, i):
+        return remote(p4s.at[kv, i], p4r.at[kv, x], p4ss.at[kv, i], p4rs.at[kv, x], s, i * 2 + c)
+
+    for kv in range(2):
+        for d in W_ROUNDS[-1]:
+            w_wait(kv, d)
+        product(kv, 1 - c, p3s)
+        for i in range(NY):
+            p3_copy(kv, i).start()
+        product(kv, c, p4s)
+
+    for kv in range(2):
+        for i in range(NY):
+            p3_copy(kv, i).wait_recv()
+            p4s[kv, i] += p3r[kv, i]
+
+            @pl.when(x == i)
+            def _(kv=kv, i=i):
+                p4r[kv, x] = p4s[kv, i]
+
+            @pl.when(x != i)
+            def _(kv=kv, i=i):
+                p4_copy(kv, i).start()
+
+    def t_copy(kv):
+        return remote(kvs.at[kv], first_block.at[kv], ts.at[kv], tr.at[kv], x * NZ + z, y * 2 + c)
+
+    for kv in range(2):
+        for i in range(NX):
+            @pl.when(x != i)
+            def _(kv=kv, i=i):
+                slot = p4r.at[kv, i]
+                remote(slot, slot, p4ss.at[kv, i], p4rs.at[kv, i], s, t).wait_recv()
+
+        total = (p4r[kv, 0] + p4r[kv, 1]) + (p4r[kv, 2] + p4r[kv, 3]) + bias[8 + kv : 9 + kv]
+        total = jnp.transpose(total)
+        if kv == 0:
+            total = jnp.transpose(rotate(total, tables))
+        kvs[kv] = total.astype(BF)
+
+        @pl.when(mine)
+        def _(kv=kv):
+            first_block[kv] = kvs[kv]
+
+        @pl.when(jnp.logical_not(mine))
+        def _(kv=kv):
+            t_copy(kv).start()
+
+    for kv in range(2):
+        @pl.when(jnp.logical_not(mine))
+        def _(kv=kv):
+            t_copy(kv).wait_recv()
+
+        forward(kv, 0)
 
     def finish():
         for d, hops in W_ONWARD.items():
@@ -253,12 +265,13 @@
                     w_copy(kv, d, hop).wait_send()
         for d in range(1, NY):
             h_copy(d).wait_send()
-        for i in range(NY):
-            p3_copy(i).wait_send()
-
-            @pl.when(x != i)
-            def _(i=i):
-                p4_copy(i).wait_send()
+        for kv in range(2):
+            for i in range(NY):
+                p3_copy(kv, i).wait_send()
+
+                @pl.when(x != i)
+                def _(kv=kv, i=i):
+                    p4_copy(kv, i).wait_send()
 
         @pl.when(mine)
         def _():
@@ -268,7 +281,8 @@
 
         @pl.when(jnp.logical_not(mine))
         def _():
-            t_copy().wait_send()
+            for kv in range(2):
+                t_copy(kv).wait_send()
 
     return finish
 
@@ -316,31 +330,35 @@
     ([25, 23, 24], [23, 24, 25, 32]),
 ]
 SINKS_AFTER = 12
+SHIFTS = sorted({shift % NS for moves in ONWARD.values() for shift, _ in moves} | {32, 48})
 SLOT = {0: 0}
 for _, group in ROUNDS:
     for j in group:
         SLOT[j] = len(SLOT)
 
 
-def attention(
-    q_ref, i_ref, o_ref,
-    buf, acc, m_ref, l_ref, column, sacc_k, sacc_v, out_k, out_v, in_k, in_v, more_k, more_v, cs, cr, ss, sr,
-):
+def block_copies(buf, cs, cr):
     s, t, x, c, y, z = coords()
-
-    def at(shift):
-        return lax.rem(s + shift + NS, NS)
 
     def copy(kv, j, shift, there):
         src, dst = buf.at[SLOT[j], kv], buf.at[SLOT[there], kv]
-        return remote(src, dst, cs.at[kv, there], cr.at[kv, there], at(shift), t)
+        return remote(src, dst, cs.at[kv, there], cr.at[kv, there], lax.rem(s + shift + NS, NS), t)
 
     def forward(kv, j):
         for shift, there in ONWARD.get(j, []):
             copy(kv, j, shift, there).start()
 
-    for kv in range(2):
-        forward(kv, 0)
+    return copy, forward
+
+
+def attention(
+    copy, forward, q_ref, i_ref, o_ref,
+    buf, acc, m_ref, l_ref, column, sacc_k, sacc_v, out_k, out_v, in_k, in_v, more_k, more_v, ss, sr,
+):
+    s, t, x, c, y, z = coords()
+
+    def at(shift):
+        return lax.rem(s + shift + NS, NS)
 
     sink_row = i_ref[...]
     for i in range(NSINK // TQ):
@@ -510,6 +528,8 @@
         pltpu.VMEM((HD, G * TQ), BF),
         pltpu.VMEM((33, 2, TQ, HD), BF),
         pltpu.VMEM((1, NSINK), jnp.int32),
+        dma((2, 33)),
+        dma((2, 33)),
     ]
     projecting = [
         pltpu.VMEM((TQ, G * HD), BF),
@@ -517,10 +537,10 @@
         pltpu.VMEM((3, TQ), jnp.int32),
         pltpu.VMEM((NY, TQ, DL), BF),
         pltpu.VMEM((2, 8, 2, 16, DL), BF),
-        pltpu.VMEM((NY, 2, TQ, HD), F32),
-        pltpu.VMEM((NY, 2, TQ, HD), F32),
-        pltpu.VMEM((NY, 2, TQ, HD), F32),
-        pltpu.VMEM((NX, 2, TQ, HD), F32),
+        pltpu.VMEM((2, NY, TQ, HD), F32),
+        pltpu.VMEM((2, NY, TQ, HD), F32),
+        pltpu.VMEM((2, NY, TQ, HD), F32),
+        pltpu.VMEM((2, NX, TQ, HD), F32),
         pltpu.VMEM((16, TQ), F32),
         pltpu.VMEM((16, HD), F32),
         pltpu.VMEM((2, TQ, HD), BF),
@@ -529,14 +549,14 @@
         dma((NY,)),
         dma((2, NZ)),
         dma((2, NZ)),
-        dma((NY,)),
-        dma((NY,)),
-        dma((NX,)),
-        dma((NX,)),
+        dma((2, NY)),
+        dma((2, NY)),
+        dma((2, NX)),
+        dma((2, NX)),
         dma((2, NY)),
         dma((2,)),
-        dma,
-        dma,
+        dma((2,)),
+        dma((2,)),
     ]
     attending = [
         pltpu.VMEM((HD, G * TQ), F32),
@@ -547,13 +567,15 @@
         pltpu.VMEM((HD, NSINK), F32),
     ]
     attending += [pltpu.VMEM((NSINK, HD), BF), pltpu.VMEM((HD, NSINK), BF)] * 3
-    attending += [dma((2, 33)), dma((2, 33)), dma((3, 2)), dma((3, 2))]
+    attending += [dma((3, 2)), dma((3, 2))]
 
     def whole(*refs):
         inputs, o_ref, refs = refs[:6], refs[6], refs[7:]
         (turned, buf, sinks), refs = refs[:3], refs[3:]
-        finish = project(*inputs, turned, buf.at[0], sinks, *refs[: len(projecting)])
-        attention(turned, sinks, o_ref, buf, *refs[len(projecting) :])
+        (cs, cr), refs = refs[:2], refs[2:]
+        copy, forward = block_copies(buf, cs, cr)
+        finish = project(forward, *inputs, turned, buf.at[0], sinks, *refs[: len(projecting)])
+        attention(copy, forward, turned, sinks, o_ref, buf, *refs[len(projecting) :])
         finish()
 
     return pl.pallas_call(

time: 102 us -> 97.4 us (0.955)
  Pallas kernels: 100 us -> 95.2 us
    pallas_call x1, Pallas kernels: 100 us -> 95.2 us  [local(): pl.pallas_call(whole, out_shape=jax.ShapeDtypeStruct((TQ, G * HD), BF), i...]
where the time goes in v4:
time: 97.4 us; the launch traced here: 96.9 us
  Pallas kernels  95.2 us (98%)
  local copies, waits for them, and re-layouts  1.67 us (2%)
    pallas_call x1, Pallas kernels, local(): pl.pallas_call(whole, out_shape=jax.ShapeDtypeStruct((TQ, G * HD), BF), i...  95.2 us

profile of v4, /device:TPU:24, one launch (start us, length us, event | category | flops | bytes accessed | tf_op | source)
XLA Modules:
  0.0 96.9 jit_solution(11753239271765667103)
XLA Ops:
  0.0 95.2 %windowed.1 = bf16[128,1024]{1,0:T(8,128)(2,1)} custom-call(bf16[128,1024]{1,0:T(8,128)(2,1)} %refs_0_.1, bf16[128,1024]{1,0:T(8,128)(2,1)} %refs_1_.1, bf16[2,16,1024]{2,1,0:T(8,128)(2,1)} %bitcast.2, bf16[2,128]{1,0:T(2,128)(2,1)} %refs_3_.1, s32[3,128]{1,0:T(4,128)} %refs_4_.1, s32[1,512]{1,0:T(1,128)} %bitcast.3), custom_call_target="tpu_custom_call" | custom-call | flops 3019898880 | bytes 1048576 | tf_op jit(solution)/shard_map/windowed/pallas_call | solution.py:581
  95.2 1.7 %copy.8 = bf16[128,1024]{1,0:T(8,128)(2,1)} copy(bf16[128,1024]{1,0:T(8,128)(2,1)} %windowed.1) | data formatting | bytes 524288

commit v5 on v4

--- a/solution.py
+++ b/solution.py
@@ -297,20 +297,21 @@
     4: [(1, 5), (16, 20)],
     5: [(1, 6), (16, 21)],
     6: [(1, 7), (16, 22)],
-    7: [(1, 8), (16, 23)],
-    8: [(16, 24)],
+    7: [(16, 23)],
     15: [(-1, 14)],
     14: [(-1, 13)],
     13: [(-1, 12)],
     12: [(-1, 11)],
     11: [(-1, 10)],
     10: [(-1, 9)],
+    9: [(-1, 8)],
     31: [(-1, 30)],
     30: [(-1, 29)],
     29: [(-1, 28)],
     28: [(-1, 27)],
     27: [(-1, 26)],
     26: [(-1, 25)],
+    25: [(-1, 24)],
 }
 ROUNDS = [
     ([1, 16], [1, 16]),
@@ -325,11 +326,13 @@
     ([20], [20, 28]),
     ([7, 10, 27], [7, 10]),
     ([21], [21, 27]),
-    ([8, 9, 26], [8, 9]),
+    ([9, 26], [9]),
     ([22], [22, 26]),
-    ([25, 23, 24], [23, 24, 25, 32]),
+    ([8, 25], [8]),
+    ([23], [23, 25]),
+    ([24], [24, 32]),
 ]
-SINKS_AFTER = 12
+SINKS_AFTER = 14
 SHIFTS = sorted({shift % NS for moves in ONWARD.values() for shift, _ in moves} | {32, 48})
 SLOT = {0: 0}
 for _, group in ROUNDS:

time: 97.4 us -> 95.9 us (0.985)
  Pallas kernels: 95.2 us -> 94.1 us
    pallas_call x1, Pallas kernels: 95.2 us -> 94.1 us  [local(): pl.pallas_call(whole, out_shape=jax.ShapeDtypeStruct((TQ, G * HD), BF), i...]
where the time goes in v5:
time: 95.9 us; the launch traced here: 95.8 us
  Pallas kernels  94.1 us (98%)
  local copies, waits for them, and re-layouts  1.67 us (2%)
    pallas_call x1, Pallas kernels, local(): pl.pallas_call(whole, out_shape=jax.ShapeDtypeStruct((TQ, G * HD), BF), i...  94.1 us

profile of v5, /device:TPU:24, one launch (start us, length us, event | category | flops | bytes accessed | tf_op | source)
XLA Modules:
  0.0 95.8 jit_solution(14673265231995753732)
XLA Ops:
  0.0 94.1 %windowed.1 = bf16[128,1024]{1,0:T(8,128)(2,1)} custom-call(bf16[128,1024]{1,0:T(8,128)(2,1)} %refs_0_.1, bf16[128,1024]{1,0:T(8,128)(2,1)} %refs_1_.1, bf16[2,16,1024]{2,1,0:T(8,128)(2,1)} %bitcast.2, bf16[2,128]{1,0:T(2,128)(2,1)} %refs_3_.1, s32[3,128]{1,0:T(4,128)} %refs_4_.1, s32[1,512]{1,0:T(1,128)} %bitcast.3), custom_call_target="tpu_custom_call" | custom-call | flops 3019898880 | bytes 1048576 | tf_op jit(solution)/shard_map/windowed/pallas_call | solution.py:584
  94.1 1.7 %copy.8 = bf16[128,1024]{1,0:T(8,128)(2,1)} copy(bf16[128,1024]{1,0:T(8,128)(2,1)} %windowed.1) | data formatting | bytes 524288

commit v6 on v5

--- a/solution.py
+++ b/solution.py
@@ -317,7 +317,7 @@
     ([1, 16], [1, 16]),
     ([2, 15, 32], [2, 15]),
     ([3, 14, 31], [3, 14]),
-    ([17], [17, 31]),
+    ([17], [17, 31, 32]),
     ([4, 13, 30], [4, 13]),
     ([18], [18, 30]),
     ([5, 12, 29], [5, 12]),
@@ -330,7 +330,7 @@
     ([22], [22, 26]),
     ([8, 25], [8]),
     ([23], [23, 25]),
-    ([24], [24, 32]),
+    ([24], [24]),
 ]
 SINKS_AFTER = 14
 SHIFTS = sorted({shift % NS for moves in ONWARD.values() for shift, _ in moves} | {32, 48})

time: 95.9 us -> 96.4 us (level)
  no operation moved by 1% of the time
where the time goes in v6:
time: 96.4 us; the launch traced here: 96.3 us
  Pallas kernels  94.6 us (98%)
  local copies, waits for them, and re-layouts  1.67 us (2%)
    pallas_call x1, Pallas kernels, local(): pl.pallas_call(whole, out_shape=jax.ShapeDtypeStruct((TQ, G * HD), BF), i...  94.6 us

profile of v6, /device:TPU:24, one launch (start us, length us, event | category | flops | bytes accessed | tf_op | source)
XLA Modules:
  0.0 96.3 jit_solution(1424846323152403510)
XLA Ops:
  0.0 94.6 %windowed.1 = bf16[128,1024]{1,0:T(8,128)(2,1)} custom-call(bf16[128,1024]{1,0:T(8,128)(2,1)} %refs_0_.1, bf16[128,1024]{1,0:T(8,128)(2,1)} %refs_1_.1, bf16[2,16,1024]{2,1,0:T(8,128)(2,1)} %bitcast.2, bf16[2,128]{1,0:T(2,128)(2,1)} %refs_3_.1, s32[3,128]{1,0:T(4,128)} %refs_4_.1, s32[1,512]{1,0:T(1,128)} %bitcast.3), custom_call_target="tpu_custom_call" | custom-call | flops 3019898880 | bytes 1048576 | tf_op jit(solution)/shard_map/windowed/pallas_call | solution.py:584
  94.6 1.7 %copy.8 = bf16[128,1024]{1,0:T(8,128)(2,1)} copy(bf16[128,1024]{1,0:T(8,128)(2,1)} %windowed.1) | data formatting | bytes 524288
